TPU v7x, 256 devices: a whole 4x4x8 slice. The times are simulated.
256 devices in a mesh: row: 16 (over z, core), col: 16 (over x, y).
Axes of the slice: x: 4, y: 4, z: 8, core: 2. Of those that a mesh axis runs over, the one named last changes fastest.
Arguments:
- inputs: bfloat16 [32, 1048576], P(None, ('row', 'col')), may hold values from -6 to 6
- morton_order: int32 [1048576], P(('row', 'col')), may hold values from 0 to 4095, as said below
- basis: bfloat16 [4096, 64, 256], P(('row', 'col')), may hold values from -0.375 to 0.375
- leaf_up: float32 [16, 64, 64], replicated, may hold values from -0.1875 to 0.1875
- up_transfer: float32 [16, 30, 64, 64], P('row'), may hold values from -0.5 to 0.5
- couple_leaf: bfloat16 [4096, 4, 64, 64], P(('row', 'col')), may hold values from -0.375 to 0.375
- leaf_lists: int32 [4096, 4], P(('row', 'col')), may hold values from 0 to 4095, as said below
- couple_row: bfloat16 [16, 3, 64, 64], P('row'), may hold values from -7 to 7
- row_lists: int32 [16, 3], P('row'), may hold values from 0 to 15, as said below
- near_blocks: bfloat16 [4096, 4, 256, 256], P(('row', 'col')), may hold values from -0.1875 to 0.1875
- near_offsets: int32 [4096, 4], P(('row', 'col')), may hold values from -4 to 4, as said below
Outputs:
- product: bfloat16 [32, 1048576], P(None, ('row', 'col'))
Inputs may be any that keep to these rules, and one draw needn't show every extreme that they name: `morton_order`: each device block of 4096 entries is a permutation of 0 .. 4095. `near_offsets`: the 4 offsets of a leaf are distinct. `leaf_lists`: source k of a leaf in device block (r, c) is a leaf of device block (r, (c + o_k) mod 16) of the same outer node, with o_0 = 15, o_1 = 8 and o_k = k - 1 for k >= 2, more than 4 leaves from the target in that node's cyclic leaf order. `row_lists`: the 3 sources of an outer node are distinct and differ from it.
All inputs are finite; a program needn't handle non-finite values.
Results may differ from a plain program's by a relative error of at most 0.0055.
Values may be sent and summed in bfloat16 or wider, within the bound.
No kernel may reach another device: no remote copies, remote signals or barrier semaphores. Data moves between devices by JAX's collectives and lax.ppermute only.
A program may use at most 64 MiB of HBM per device.

v0:
```python
import jax
import jax.numpy as jnp
from jax import lax
from jax.sharding import PartitionSpec as P

REACH = 4


def swapped(array, axis, bit):
    return lax.ppermute(array, axis, [(i, i ^ 1 << bit) for i in range(lax.axis_size(axis))])


def extended_2(cells, sides, width):
    for axis, dim in sides:
        count = lax.axis_size(axis)
        ends = count - 1
        head = lax.slice_in_dim(cells, 0, width, axis=dim)
        tail = lax.slice_in_dim(cells, cells.shape[dim] - width, cells.shape[dim], axis=dim)
        cells = jnp.concatenate(
            [
                lax.ppermute(tail, axis, [(i, (i + 1) % count) for i in range(ends)]),
                cells,
                lax.ppermute(head, axis, [((i + 1) % count, i) for i in range(ends)]),
            ],
            axis=dim,
        )
    return cells


def local(
    inputs,
    morton_order,
    basis,
    leaf_up,
    up_transfer,
    couple_leaf,
    leaf_lists,
    couple_row,
    row_lists,
    near_blocks,
    near_offsets,
):
    highest = lax.Precision.HIGHEST
    rhs_count = inputs.shape[0]
    leaf_count, rank_size, leaf_points = basis.shape
    ordered = jnp.take(inputs, morton_order, axis=1)
    leaves = ordered.reshape(rhs_count, leaf_count, leaf_points)
    multipoles = jnp.einsum(
        "nlp,lrp->lnr", leaves, basis, preferred_element_type=jnp.float32
    ).astype(jnp.bfloat16)
    device_pole = jnp.einsum(
        "lns,lst->nt", multipoles.astype(jnp.float32), leaf_up, precision=highest
    )
    col_count = lax.axis_size("col")
    col_depth = col_count.bit_length() - 1
    col_place = lax.axis_index("col")
    transfers = up_transfer[0]

    def transfer_at(height):
        heap_first = 2 * col_count - 2 * (col_count >> height)
        return transfers[heap_first + (col_place >> height)]

    climbing = device_pole
    for height in range(col_depth):
        lifted = jnp.dot(climbing, transfer_at(height), precision=highest)
        climbing = lifted + swapped(lifted, "col", height)
    row_wire = climbing.astype(jnp.bfloat16).reshape(1, rhs_count * rank_size)
    row_poles = lax.all_gather(row_wire, "row", axis=0, tiled=True).reshape(
        -1, rhs_count, rank_size
    )
    row_picked = row_poles[row_lists[0]]
    row_local = jnp.einsum(
        "kns,kst->nt", row_picked, couple_row[0], preferred_element_type=jnp.float32
    )
    downward = row_local
    for height in reversed(range(col_depth)):
        downward = jnp.einsum("nt,st->ns", downward, transfer_at(height), precision=highest)
    row_leaves = leaf_count * col_count
    list_slots = leaf_lists.shape[1]
    local_lists = (leaf_lists - lax.axis_index("row") * row_leaves).reshape(-1)
    flat_poles = multipoles.reshape(leaf_count, rhs_count * rank_size)
    everyone = lax.all_gather(flat_poles, "col", axis=0, tiled=True)
    leaf_picked = everyone[local_lists]
    leaf_picked = leaf_picked.reshape(leaf_count, list_slots, rhs_count, rank_size)
    coupled = jnp.einsum(
        "lkns,lkst->lnt", leaf_picked, couple_leaf, preferred_element_type=jnp.float32
    )
    pushed = jnp.einsum("ns,lts->lnt", downward, leaf_up, precision=highest)
    leaf_local = (coupled + pushed).astype(jnp.bfloat16)
    far_part = jnp.einsum("lnr,lrp->nlp", leaf_local, basis, preferred_element_type=jnp.float32)
    extended = extended_2(ordered, ((("row", "col"), 1),), REACH * leaf_points)
    extended_leaves = extended.reshape(rhs_count, leaf_count + 2 * REACH, leaf_points)
    source_pos = jnp.arange(leaf_count, dtype=jnp.int32)[:, None] + REACH + near_offsets
    sources = extended_leaves[:, source_pos]
    near_part = jnp.einsum(
        "nlks,lkst->nlt", sources, near_blocks, preferred_element_type=jnp.float32
    )
    summed = (near_part + far_part).astype(jnp.bfloat16).reshape(rhs_count, -1)
    return jnp.zeros_like(summed).at[:, morton_order].set(summed)


def solution(mesh):
    return jax.shard_map(
        local,
        mesh=mesh,
        in_specs=(
            P(None, ("row", "col")),
            P(("row", "col")),
            P(("row", "col"), None, None),
            P(),
            P("row", None, None, None),
            P(("row", "col"), None, None, None),
            P(("row", "col"), None),
            P("row", None, None, None),
            P("row", None),
            P(("row", "col"), None, None, None),
            P(("row", "col"), None),
        ),
        out_specs=P(None, ("row", "col")),
        check_vma=False,
    )
```

profile of v0, /device:TPU:1, one launch (start us, length us, event | category | flops | bytes accessed | tf_op | source)
XLA Modules:
  0.0 116.9 jit_solution(15484060077949200849)
XLA Ops:
  8.1 1.4 %copy.48 = bf16[32,4096]{0,1:T(8,128)(2,1)S(1)} copy(bf16[32,4096]{1,0:T(8,128)(2,1)} %param.11) | data formatting | bytes 524288 | tf_op args[0]
  9.6 12.1 %gather_fusion = bf16[4096,32]{1,0:T(8,128)(2,1)S(1)} fusion(bf16[32,4096]{0,1:T(8,128)(2,1)S(1)} %copy.48, s32[4096]{0:T(1024)S(1)} %get-tuple-element.7), kind=kCustom, calls=%fused_computation | custom fusion | bytes 540672 | tf_op jit(solution)/shard_map/jit(_take)/gather | solution.py:46
  22.0 1.3 %convolution_convert_fusion = bf16[16,32,64]{2,1,0:T(8,128)(2,1)S(1)} fusion(bf16[16,64,256]{2,1,0:T(8,128)(2,1)} %param.13, bf16[32,16,256]{2,0,1:T(8,128)(2,1)S(1)} %copy.54, pred[16,256]{1,0:T(8,128)(4,1)S(1)} %broadcast_in_dim.33), kind=kOutput, calls=%fused_computation.13 | convolution fusion | flops 16941056 | bytes 856064 | tf_op jit(solution)/shard_map/nlp,lrp->lnr/dot_general | solution.py:48
  23.3 1.4 %convolution_bitcast_fusion.5 = f32[32,64]{1,0:T(8,128)S(1)} fusion(bf16[16,32,64]{2,1,0:T(8,128)(2,1)S(1)} %convolution_convert_fusion, f32[16,64,64]{2,1,0:T(8,128)} %param.14), kind=kOutput, calls=%fused_computation.16 | convolution fusion | flops 25165824 | bytes 335872 | tf_op jit(solution)/shard_map/lns,lst->nt/dot_general | solution.py:51
  25.6 2.2 %collective-permute-start.2 = (f32[32,64]{1,0:T(8,128)S(1)}, f32[32,64]{1,0:T(8,128)S(1)}, u32[]{:S(2)}, u32[]{:S(2)}) collective-permute-start(f32[32,64]{1,0:T(8,128)S(1)} %fusion.24), channel_id=1, source_target_pairs={{0,1},{1,0},{2,3},{3,2},{4,5},{5,4},{6,7},{7,6},{8,9},{9,8},{10,11... | collective-permute-start | bytes 24584 | tf_op jit(solution)/shard_map/ppermute | solution.py:10
  28.7 2.1 %bitcast_select_fusion = bf16[32,4096]{0,1:T(8,128)(2,1)S(1)} fusion(bf16[4096,32]{1,0:T(8,128)(2,1)S(1)} %gather_fusion, pred[4096]{0:T(1024)(128)(4,1)S(1)} %compare_and_fusion), kind=kLoop, calls=%fused_computation.17 | loop fusion | flops 131072 | bytes 528384 | tf_op jit(solution)/shard_map/jit(_take)/select_n | solution.py:46
  30.9 1.9 %collective-permute-start = (bf16[32,1024]{0,1:T(8,128)(2,1)S(1)}, bf16[32,1024]{0,1:T(8,128)(2,1)S(1)}, u32[]{:S(2)}, u32[]{:S(2)}) collective-permute-start(bf16[32,1024]{0,1:T(8,128)(2,1)S(1)} %get-tuple-element.5), channel_id=1, source_target_pairs={{0,1},{1,2},{2,3},{3,4},{4,5},{5,6},{6,7},{7,8},{8,9},{9,10},{10,1... | collective-permute-start | bytes 196616 | tf_op jit(solution)/shard_map/ppermute | solution.py:21
  32.8 7.0 %collective-permute-start.1 = (bf16[32,1024]{0,1:T(8,128)(2,1)S(1)}, bf16[32,1024]{0,1:T(8,128)(2,1)S(1)}, u32[]{:S(2)}, u32[]{:S(2)}) collective-permute-start(bf16[32,1024]{0,1:T(8,128)(2,1)S(1)} %get-tuple-element.6), channel_id=1, source_target_pairs={{1,0},{2,1},{3,2},{4,3},{5,4},{6,5},{7,6},{8,7},{9,8},{10,9},{11,1... | collective-permute-start | bytes 196616 | tf_op jit(solution)/shard_map/ppermute | solution.py:23
  41.1 4.1 %collective-permute-done.3 = f32[32,64]{1,0:T(8,128)S(1)} collective-permute-done((f32[32,64]{1,0:T(8,128)S(1)}, f32[32,64]{1,0:T(8,128)S(1)}, u32[]{:S(2)}, u32[]{:S(2)}) %collective-permute-start.3) | collective-permute-done | bytes 8224 | tf_op jit(solution)/shard_map/ppermute | solution.py:10
  46.3 2.8 %collective-permute-done.4 = f32[32,64]{1,0:T(8,128)S(1)} collective-permute-done((f32[32,64]{1,0:T(8,128)S(1)}, f32[32,64]{1,0:T(8,128)S(1)}, u32[]{:S(2)}, u32[]{:S(2)}) %collective-permute-start.4) | collective-permute-done | bytes 8224 | tf_op jit(solution)/shard_map/ppermute | solution.py:10
  49.1 0.9 fusion.13
  50.0 1.4 %collective-permute-start.5 = (f32[32,64]{1,0:T(8,128)S(1)}, f32[32,64]{1,0:T(8,128)S(1)}, u32[]{:S(2)}, u32[]{:S(2)}) collective-permute-start(f32[32,64]{1,0:T(8,128)S(1)} %fusion.13), channel_id=1, source_target_pairs={{0,8},{1,9},{2,10},{3,11},{4,12},{5,13},{6,14},{7,15},{8,0},{9,1},... | collective-permute-start | bytes 24584 | tf_op jit(solution)/shard_map/ppermute | solution.py:10
  51.8 2.4 %collective-permute-done.5 = f32[32,64]{1,0:T(8,128)S(1)} collective-permute-done((f32[32,64]{1,0:T(8,128)S(1)}, f32[32,64]{1,0:T(8,128)S(1)}, u32[]{:S(2)}, u32[]{:S(2)}) %collective-permute-start.5) | collective-permute-done | bytes 8224 | tf_op jit(solution)/shard_map/ppermute | solution.py:10
  54.3 25.2 %all-gather = bf16[16,1,2048]{2,1,0:T(2,128)(2,1)S(1)} all-gather(bf16[1,1,2048]{2,1,0:T(2,128)(2,1)S(1)} %reshape.152), channel_id=1, replica_groups=mesh['row'=16,'col'=16] {'row'}, dimensions={0}, use_global_device_ids=true | all-gather | bytes 69632 | tf_op jit(solution)/shard_map/all_gather | solution.py:68
  80.8 0.9 fusion.11
  81.7 0.9 fusion.15
  82.6 0.9 fusion.19
  83.6 0.9 convolution_bitcast_fusion.3
  85.5 2.3 %gather_fusion.2 = bf16[64,2048]{1,0:T(8,128)(2,1)S(1)} fusion(bf16[256,2048]{1,0:T(8,128)(2,1)} %all-gather.3.cloned.1.call-done, s32[1024]{0:T(1024)S(1)} %pad_clamp_fusion.1), kind=kCustom, calls=%fused_computation.2 | custom fusion | bytes 524544 | tf_op jit(solution)/shard_map/gather | solution.py:83
  88.7 2.6 %fusion.4 = bf16[16,32,64]{2,1,0:T(8,128)(2,1)S(1)} fusion(f32[16,32,64]{2,1,0:T(8,128)S(1)} %convolution_bitcast_fusion.2, f32[32,64,1]{1,0,2:T(8,128)S(1)} %convolution_bitcast_fusion.3, f32[16,64,64]{2,1,0:T(8,128)} %param.14), kind=kOutput, calls=%fused_computation.12 | convolution fusion | flops 25231360 | bytes 466944 | tf_op jit(solution)/shard_map/ns,lts->lnt/dot_general | solution.py:88
  91.3 1.3 %fusion.49 = f32[16,32,256]{2,1,0:T(8,128)S(1)} fusion(bf16[16,32,64]{2,1,0:T(8,128)(2,1)S(1)} %fusion.4, bf16[16,64,256]{2,1,0:T(8,128)(2,1)} %param.13), kind=kOutput, calls=%fused_computation.76 | convolution fusion | flops 16777216 | bytes 1114112 | tf_op jit(solution)/shard_map/lnr,lrp->nlp/dot_general | solution.py:90
  92.6 4.8 %fusion.3 = bf16[16,4,8,256]{3,2,1,0:T(8,128)(2,1)S(1)} fusion(f32[16,32,256]{2,1,0:T(8,128)S(1)} %fusion.49, bf16[32,16,4,256]{3,0,2,1:T(8,128)(2,1)S(1)} %bitcast.87, bf16[16,4,256,256]{3,2,1,0:T(8,128)(2,1)} %param.20), kind=kOutput, calls=%fused_computation.10 | convolution fusion | flops 268697600 | bytes 10223616 | tf_op jit(solution)/shard_map/nlks,lkst->nlt/dot_general | solution.py:95
  97.9 11.1 %scatter_custom_fusion = bf16[32,4096]{0,1:T(8,128)(2,1)S(1)} fusion(s32[4096]{0:T(1024)S(1)} %get-tuple-element.8, bf16[4096,32]{1,0:T(8,128)(2,1)S(1)} %copy.57, bf16[]{:T(256)} %constant.19.clone.1), kind=kCustom, calls=%fused_computation.18 | custom fusion | bytes 262146 | tf_op jit(solution)/shard_map/scatter | solution.py:99
  109.0 1.0 copy.58
  (55 shorter events, 10.0 us)
Async XLA Ops:
  6.5 81.9 %copy-start = (bf16[16,4,64,64]{3,2,1,0:T(8,128)(2,1)S(1)}, bf16[16,4,64,64]{3,2,1,0:T(8,128)(2,1)}, u32[]{:S(2)}) copy-start(bf16[16,4,64,64]{3,2,1,0:T(8,128)(2,1)} %param.16) | copy-start | bytes 1572868
  6.5 33.2 %copy-start.4 = (s32[1,3]{1,0:T(1,128)S(1)}, s32[1,3]{1,0:T(1,128)}, u32[]{:S(2)}) copy-start(s32[1,3]{1,0:T(1,128)} %param.19) | copy-start | bytes 40
  6.5 33.3 %copy-start.2 = (s32[16,4]{0,1:T(4,128)S(1)}, s32[16,4]{0,1:T(4,128)}, u32[]{:S(2)}) copy-start(s32[16,4]{0,1:T(4,128)} %param.17) | copy-start | bytes 772
  6.5 33.5 %copy-start.3 = (s32[16,4]{0,1:T(4,128)S(1)}, s32[16,4]{0,1:T(4,128)}, u32[]{:S(2)}) copy-start(s32[16,4]{0,1:T(4,128)} %param.21) | copy-start | bytes 772
  6.5 74.0 %copy-start.1 = (bf16[1,3,64,64]{3,2,1,0:T(8,128)(2,1)S(1)}, bf16[1,3,64,64]{3,2,1,0:T(8,128)(2,1)}, u32[]{:S(2)}) copy-start(bf16[1,3,64,64]{3,2,1,0:T(8,128)(2,1)} %param.18) | copy-start | bytes 73732
  6.5 79.0 %all-gather.3.cloned.1.call-start = ((), (), s32[]{:S(2)}) async-start(), calls=%async_computation | async-start | bytes 1114112 | tf_op jit(solution)/shard_map/all_gather | solution.py:82
  25.6 14.4 %collective-permute-start.2 = (f32[32,64]{1,0:T(8,128)S(1)}, f32[32,64]{1,0:T(8,128)S(1)}, u32[]{:S(2)}, u32[]{:S(2)}) collective-permute-start(f32[32,64]{1,0:T(8,128)S(1)} %fusion.24), channel_id=1, source_target_pairs={{0,1},{1,0},{2,3},{3,2},{4,5},{5,4},{6,7},{7,6},{8,9},{9,8},{10,11... | collective-permute-start | bytes 24584 | tf_op jit(solution)/shard_map/ppermute | solution.py:10
  30.9 53.6 %collective-permute-start = (bf16[32,1024]{0,1:T(8,128)(2,1)S(1)}, bf16[32,1024]{0,1:T(8,128)(2,1)S(1)}, u32[]{:S(2)}, u32[]{:S(2)}) collective-permute-start(bf16[32,1024]{0,1:T(8,128)(2,1)S(1)} %get-tuple-element.5), channel_id=1, source_target_pairs={{0,1},{1,2},{2,3},{3,4},{4,5},{5,6},{6,7},{7,8},{8,9},{9,10},{10,1... | collective-permute-start | bytes 196616 | tf_op jit(solution)/shard_map/ppermute | solution.py:21
  32.8 51.8 %collective-permute-start.1 = (bf16[32,1024]{0,1:T(8,128)(2,1)S(1)}, bf16[32,1024]{0,1:T(8,128)(2,1)S(1)}, u32[]{:S(2)}, u32[]{:S(2)}) collective-permute-start(bf16[32,1024]{0,1:T(8,128)(2,1)S(1)} %get-tuple-element.6), channel_id=1, source_target_pairs={{1,0},{2,1},{3,2},{4,3},{5,4},{6,5},{7,6},{8,7},{9,8},{10,9},{11,1... | collective-permute-start | bytes 196616 | tf_op jit(solution)/shard_map/ppermute | solution.py:23
  41.0 4.2 %collective-permute-start.3 = (f32[32,64]{1,0:T(8,128)S(1)}, f32[32,64]{1,0:T(8,128)S(1)}, u32[]{:S(2)}, u32[]{:S(2)}) collective-permute-start(f32[32,64]{1,0:T(8,128)S(1)} %fusion.21), channel_id=1, source_target_pairs={{0,2},{1,3},{2,0},{3,1},{4,6},{5,7},{6,4},{7,5},{8,10},{9,11},{10,... | collective-permute-start | bytes 24584 | tf_op jit(solution)/shard_map/ppermute | solution.py:10
  46.0 3.1 %collective-permute-start.4 = (f32[32,64]{1,0:T(8,128)S(1)}, f32[32,64]{1,0:T(8,128)S(1)}, u32[]{:S(2)}, u32[]{:S(2)}) collective-permute-start(f32[32,64]{1,0:T(8,128)S(1)} %fusion.17), channel_id=1, source_target_pairs={{0,4},{1,5},{2,6},{3,7},{4,0},{5,1},{6,2},{7,3},{8,12},{9,13},{10,... | collective-permute-start | bytes 24584 | tf_op jit(solution)/shard_map/ppermute | solution.py:10
  50.0 4.2 %collective-permute-start.5 = (f32[32,64]{1,0:T(8,128)S(1)}, f32[32,64]{1,0:T(8,128)S(1)}, u32[]{:S(2)}, u32[]{:S(2)}) collective-permute-start(f32[32,64]{1,0:T(8,128)S(1)} %fusion.13), channel_id=1, source_target_pairs={{0,8},{1,9},{2,10},{3,11},{4,12},{5,13},{6,14},{7,15},{8,0},{9,1},... | collective-permute-start | bytes 24584 | tf_op jit(solution)/shard_map/ppermute | solution.py:10
Sparse Core Ops, SparseCore 0:
  28.8 50.0 all-gather.2
where the time goes:
time: 118 us; the launch traced here: 117 us
  local copies, waits for them, and re-layouts  32.6 us (28%)
  blocking collectives  25.2 us (21%)
  matrix products  19.1 us (16%)
  between operations  13.8 us (12%)
  starting transfers between devices  12.7 us (11%)
  waiting for transfers between devices  9.34 us (8%)
  other arithmetic  4.1 us (3%)
    all_gather x1, blocking collectives, local(): lax.all_gather(row_wire, 'row', axis=0, tiled=True)  25.2 us
    gather x2, local copies, waits for them, and re-layouts, local(): ordered = jnp.take(inputs, morton_order, axis=1)  12.5 us
    scatter x2, local copies, waits for them, and re-layouts, local(): return jnp.zeros_like(summed).at[:, morton_order].set(summed)  12.2 us
    ppermute x4, waiting for transfers between devices, swapped(): lax.ppermute(array, axis, [(i, i ^ 1 << bit) for i in range(lax.axis_size...  9.29 us
    ppermute x1, starting transfers between devices, extended_2(): lax.ppermute(head, axis, [((i + 1) % count, i) for i in range(ends)])  6.96 us
    dot_general x1, matrix products, local(): jnp.einsum('nlks,lkst->nlt', sources, near_blocks, preferred_element_type...  4.78 us
    ppermute x4, starting transfers between devices, swapped(): lax.ppermute(array, axis, [(i, i ^ 1 << bit) for i in range(lax.axis_size...  3.81 us
    dot_general x4, matrix products, local(): jnp.einsum('nt,st->ns', downward, transfer_at(height), precision=highest)  3.7 us
  transfers between devices with their start and end apart: 7, of which 3 were waited for; matrix products, arithmetic and copies ran while one was open for 11% of the time, Pallas kernels for 0%

commit v1 on v0

v1 whole, which is shorter than its diff:
```python
import jax
import jax.numpy as jnp
from jax import lax
from jax.experimental import pallas as pl
from jax.experimental.pallas import tpu as pltpu
from jax.sharding import PartitionSpec as P

REACH = 4
BF = jnp.bfloat16
F32 = jnp.float32
HIGHEST = lax.Precision.HIGHEST
VMEM = pl.BlockSpec(memory_space=pltpu.VMEM)
SMEM = pl.BlockSpec(memory_space=pltpu.SMEM)
ANY = pl.BlockSpec(memory_space=pl.ANY)
LANES = 128
GROUP = 2
AHEAD = 8


def in_hbm(value):
    return pltpu.with_memory_space_constraint(value, pltpu.HBM)


def mm(a, b):
    return jnp.dot(a, b, preferred_element_type=F32)


def mm_t(a, b):
    return lax.dot_general(a, b, (((1,), (1,)), ((), ())), preferred_element_type=F32)


def halves(value):
    high = value.astype(BF)
    return high, (value - high.astype(F32)).astype(BF)


def one_hot(low, size):
    rows = lax.broadcasted_iota(jnp.int32, (size, low.shape[1]), 0).astype(BF)
    wanted = jnp.broadcast_to(low.astype(BF), rows.shape)
    return jnp.where(rows == wanted, jnp.ones_like(rows), jnp.zeros_like(rows))


def up_kernel(
    place, x_hbm, order_hbm, basis_hbm, leaf_up_hbm, up, lifted, first_out, second_out, poles, ordered, chain,
    x, order, basis, leaf_up, steps, sems,
):
    leaf_count, rank, points = basis.shape
    rhs = x.shape[0]
    depth = steps.shape[0]
    half = leaf_count // 2
    edge = 2 * REACH
    col, cols = place[0], lifted.shape[0]
    first = [
        pltpu.make_async_copy(order_hbm, order, sems.at[0]),
        pltpu.make_async_copy(x_hbm, x, sems.at[1]),
    ]
    for h in range(depth):
        node = 2 * cols - 2 * (cols >> h) + (col >> h)
        first.append(pltpu.make_async_copy(up.at[0, node], steps.at[h], sems.at[4 + h]))
    second = [pltpu.make_async_copy(basis_hbm, basis, sems.at[2])]
    third = [pltpu.make_async_copy(leaf_up_hbm, leaf_up, sems.at[3])]
    for copy in first + second + third:
        copy.start()
    for copy in first:
        copy.wait()
    whole = steps[0]
    for h in range(1, depth):
        whole = jnp.dot(whole, steps[h], precision=HIGHEST, preferred_element_type=F32)
    chain[...] = whole
    slabs = jnp.concatenate(
        [x[:, a * points : (a + 1) * points] for a in range(leaf_count)], axis=0
    )
    leaves = []
    for i in range(leaf_count):
        where = order[:, i * points : (i + 1) * points]
        low = where & (points - 1)
        high = jnp.broadcast_to(where // points, (8, points))
        picked = mm(slabs, one_hot(low, points)).reshape(leaf_count, rhs // 8, 8, points)
        total = picked[0]
        for a in range(1, leaf_count):
            total = jnp.where((high == a)[None], picked[a], total)
        leaf = total.reshape(rhs, points).astype(BF)
        ordered[2 * i] = leaf[:, :LANES]
        ordered[2 * i + 1] = leaf[:, LANES:]
        leaves.append(leaf)
    for copy in second:
        copy.wait()
    moments = [mm_t(leaves[i], basis[i]).astype(BF) for i in range(leaf_count)]
    pairs = [jnp.concatenate(moments[i : i + 2], axis=1) for i in range(0, leaf_count, 2)]
    for q in range(half):
        poles[q] = pairs[q]
        first_out[edge + q] = pairs[q]
        second_out[edge + q] = pairs[q]
    for copy in third:
        copy.wait()
    up_high, up_low = halves(leaf_up[...].reshape(leaf_count * rank, rank))
    every = jnp.concatenate(pairs, axis=1)
    top = mm(every, up_high) + mm(every, up_low)
    top = jnp.dot(top, whole, precision=HIGHEST, preferred_element_type=F32)
    packed = jnp.concatenate([top[: rhs // 2], top[rhs // 2 :]], axis=1)
    for c in range(cols):
        lifted[c] = packed
    odd = (col & 1) == 1
    head, tail = ordered[:edge], ordered[2 * leaf_count - edge :]
    first_out[:edge] = jnp.where(odd, tail, head)
    second_out[:edge] = jnp.where(odd, head, tail)


def up_call(place, inputs, order, basis, leaf_up, up_transfer, cols):
    rhs = inputs.shape[0]
    leaf_count, rank, points = basis.shape
    depth = cols.bit_length() - 1
    shape = jax.ShapeDtypeStruct
    half = leaf_count // 2
    sent = shape((2 * REACH + half, rhs, LANES), BF)
    return pl.pallas_call(
        up_kernel,
        out_shape=(
            shape((cols, rhs // 2, LANES), F32),
            sent,
            sent,
            shape((half, rhs, LANES), BF),
            shape((2 * leaf_count, rhs, LANES), BF),
            shape((rank, rank), F32),
        ),
        in_specs=[SMEM] + [ANY] * 5,
        out_specs=(VMEM,) * 6,
        scratch_shapes=[
            pltpu.VMEM(inputs.shape, BF),
            pltpu.VMEM(order.shape, order.dtype),
            pltpu.VMEM(basis.shape, BF),
            pltpu.VMEM(leaf_up.shape, F32),
            pltpu.VMEM((depth, rank, rank), F32),
            pltpu.SemaphoreType.DMA((4 + depth,)),
        ],
        compiler_params=pltpu.CompilerParams(vmem_limit_bytes=24 << 20),
        cost_estimate=pl.CostEstimate(flops=1 << 32, bytes_accessed=3 << 20, transcendentals=0),
        name="up",
    )(place, in_hbm(inputs), in_hbm(order), in_hbm(basis), in_hbm(leaf_up), in_hbm(up_transfer))


def near_kernel(place, offsets, ordered, first, second, blocks_hbm, near, extended, blocks, sems):
    leaf_count, count, points, _ = blocks.shape
    col, row, rows, cols = place[0], place[1], place[2], place[3]
    edge = 2 * REACH
    group = leaf_count // sems.shape[0]
    fetched = [
        pltpu.make_async_copy(
            blocks_hbm.at[i : i + group], blocks.at[i : i + group], sems.at[i // group]
        )
        for i in range(0, leaf_count, group)
    ]
    for copy in fetched[:AHEAD]:
        copy.start()
    odd = (col & 1) == 1
    lowest = (col == 0) & (row == 0)
    highest = (col == cols - 1) & (row == rows - 1)
    before = jnp.where(odd, second[:edge], first[:edge])
    after = jnp.where(odd, first[:edge], second[:edge])
    extended[edge : edge + 2 * leaf_count] = ordered[...]
    extended[:edge] = jnp.where(lowest, jnp.zeros_like(before), before)
    extended[edge + 2 * leaf_count :] = jnp.where(highest, jnp.zeros_like(after), after)
    for i in range(leaf_count):
        if i % group == 0:
            fetched[i // group].wait()
            if i // group + AHEAD < len(fetched):
                fetched[i // group + AHEAD].start()
        parts = []
        for k in range(count):
            at = 2 * (i + REACH + offsets[k, i])
            parts += [extended[at], extended[at + 1]]
        near[i] = mm(jnp.concatenate(parts, axis=1), blocks[i].reshape(count * points, points))


def near_call(place, offsets, ordered, first, second, near_blocks):
    leaf_count, _, points, _ = near_blocks.shape
    rhs = ordered.shape[1]
    return pl.pallas_call(
        near_kernel,
        out_shape=jax.ShapeDtypeStruct((leaf_count, rhs, points), F32),
        in_specs=[SMEM, SMEM] + [VMEM] * 3 + [ANY],
        out_specs=VMEM,
        scratch_shapes=[
            pltpu.VMEM((2 * leaf_count + 4 * REACH, rhs, LANES), BF),
            pltpu.VMEM(near_blocks.shape, BF),
            pltpu.SemaphoreType.DMA((leaf_count // GROUP,)),
        ],
        compiler_params=pltpu.CompilerParams(vmem_limit_bytes=24 << 20),
        cost_estimate=pl.CostEstimate(flops=1 << 30, bytes_accessed=10 << 20, transcendentals=0),
        name="near",
    )(place, offsets, ordered, first, second, in_hbm(near_blocks))


def down_kernel(
    place, lists, row_lists, first, second, around, p1, p3, couple_hbm, rows, couple_row, chain, leaf_up,
    basis, near, order, out, poles, couple, spread, marks, sem,
):
    leaf_count, rank, points = basis.shape
    rhs = near.shape[1]
    slots = couple.shape[1]
    edge = 2 * REACH
    col, cols = place[0], place[3]
    fetched = pltpu.make_async_copy(couple_hbm, couple, sem)
    fetched.start()
    odd = (col & 1) == 1
    poles[0] = jnp.where(odd, second[edge:], first[edge:])
    poles[2] = jnp.where(odd, first[edge:], second[edge:])
    poles[1] = p1[...]
    poles[3] = p3[...]

    @pl.when(col == 0)
    def _():
        poles[0] = around[...]

    @pl.when(col == cols - 1)
    def _():
        poles[2] = around[...]

    for i in range(leaf_count):
        where = order[:, i * points : (i + 1) * points]
        marks[:, i * points : (i + 1) * points] = one_hot(where & (points - 1), points)
    joined = []
    for i in range(leaf_count):
        parts = []
        for k in range(slots):
            source = lists[k, i] & (leaf_count - 1)
            pair = poles[k, source // 2]
            parts.append(jnp.where((source & 1) == 1, pair[:, rank:], pair[:, :rank]))
        joined.append(jnp.concatenate(parts, axis=1))
    sources = []
    for k in range(couple_row.shape[1]):
        packed = rows[row_lists[0, k]]
        sources.append(jnp.concatenate([packed[:, :rank], packed[:, rank:]], axis=0))
    local_row = mm(
        jnp.concatenate(sources, axis=1), couple_row[0].reshape(len(sources) * rank, rank)
    )
    fetched.wait()
    sides = [mm(joined[i], couple[i].reshape(slots * rank, rank)) for i in range(leaf_count)]
    downward = lax.dot_general(
        local_row, chain[...], (((1,), (1,)), ((), ())), precision=HIGHEST, preferred_element_type=F32
    )
    down_high, down_low = halves(downward)
    up_high, up_low = halves(leaf_up[...].reshape(leaf_count * rank, rank))
    both = mm_t(jnp.concatenate([down_high, down_low], axis=0), up_high)
    pushed = both[:rhs] + both[rhs:] + mm_t(down_high, up_low)
    leaf_local = (jnp.concatenate(sides, axis=1) + pushed).astype(BF)
    fars = [mm(leaf_local[:, i * rank : (i + 1) * rank], basis[i]) for i in range(leaf_count)]
    for i in range(leaf_count):
        high = (order[:, i * points : (i + 1) * points] // points).astype(BF)
        high = jnp.broadcast_to(high, (rhs, points))
        summed = (near[i] + fars[i]).astype(BF)
        for a in range(leaf_count):
            spread[a * rhs : (a + 1) * rhs, i * points : (i + 1) * points] = jnp.where(
                high == a, summed, jnp.zeros_like(summed)
            )
    total = mm_t(spread[...], marks[...]).astype(BF)
    for a in range(leaf_count):
        out[:, a * points : (a + 1) * points] = total[a * rhs : (a + 1) * rhs]


def down_call(
    place, lists, row_lists, first, second, around, p1, p3, couple, row_poles, couple_row, chain, leaf_up,
    basis, near, order,
):
    leaf_count, rank, points = basis.shape
    rhs = near.shape[1]
    return pl.pallas_call(
        down_kernel,
        out_shape=jax.ShapeDtypeStruct((rhs, leaf_count * points), BF),
        in_specs=[SMEM] * 3 + [VMEM] * 5 + [ANY] + [VMEM] * 7,
        out_specs=VMEM,
        scratch_shapes=[
            pltpu.VMEM((couple.shape[1], *p1.shape), BF),
            pltpu.VMEM(couple.shape, BF),
            pltpu.VMEM((leaf_count * rhs, leaf_count * points), BF),
            pltpu.VMEM((points, leaf_count * points), BF),
            pltpu.SemaphoreType.DMA,
        ],
        compiler_params=pltpu.CompilerParams(vmem_limit_bytes=24 << 20),
        cost_estimate=pl.CostEstimate(flops=1 << 30, bytes_accessed=3 << 20, transcendentals=0),
        name="down",
    )(
        place, lists, row_lists, first, second, around, p1, p3, in_hbm(couple), row_poles, couple_row,
        chain, leaf_up, basis, near, order,
    )


def local(
    inputs,
    morton_order,
    basis,
    leaf_up,
    up_transfer,
    couple_leaf,
    leaf_lists,
    couple_row,
    row_lists,
    near_blocks,
    near_offsets,
):
    cols = lax.axis_size("col")
    rows = lax.axis_size("row")
    count = rows * cols
    place = jnp.stack([lax.axis_index("col"), lax.axis_index("row"), rows, cols]).astype(jnp.int32)
    order = morton_order.reshape(1, -1)
    lifted, first, second, poles, ordered, chain = up_call(
        place, inputs, order, basis, leaf_up, up_transfer, cols
    )
    everyone = lax.all_to_all(lifted, "col", 0, 0, tiled=True)

    def swap(value, start):
        pairs = [(b, (b + 1) % count) for b in range(start, count, 2)]
        return lax.ppermute(value, ("row", "col"), pairs + [(b, a) for a, b in pairs])

    def from_peer(value, away):
        return lax.ppermute(value, "col", [((c + away) % cols, c) for c in range(cols)])

    first = swap(first, 1)
    row_wire = everyone.sum(axis=0).astype(BF)
    row_wire = jnp.broadcast_to(row_wire[None], (rows,) + row_wire.shape)
    row_poles = lax.all_to_all(row_wire, "row", 0, 0, tiled=True)
    second = swap(second, 0)
    p1 = from_peer(poles, cols // 2)
    p3 = from_peer(poles, 2)
    turn = [(((r + 1) % rows) * cols, r * cols) for r in range(rows)]
    turn += [(r * cols + cols - 1, ((r + 1) % rows) * cols + cols - 1) for r in range(rows)]
    around = lax.ppermute(first[2 * REACH :], ("row", "col"), turn)
    near = near_call(place, near_offsets.T, ordered, first, second, near_blocks)
    return down_call(
        place, leaf_lists.T, row_lists, first, second, around, p1, p3, couple_leaf, row_poles, couple_row,
        chain, leaf_up, basis, near, order,
    )


def solution(mesh):
    return jax.shard_map(
        local,
        mesh=mesh,
        in_specs=(
            P(None, ("row", "col")),
            P(("row", "col")),
            P(("row", "col"), None, None),
            P(),
            P("row", None, None, None),
            P(("row", "col"), None, None, None),
            P(("row", "col"), None),
            P("row", None, None, None),
            P("row", None),
            P(("row", "col"), None, None, None),
            P(("row", "col"), None),
        ),
        out_specs=P(None, ("row", "col")),
        check_vma=False,
    )
```

time: 118 us -> 45.6 us (0.39)
  local copies, waits for them, and re-layouts: 32.6 us -> 0.69 us
  blocking collectives: 25.2 us -> 0 us
  matrix products: 19.1 us -> 0 us
  starting transfers between devices: 12.7 us -> 29.5 us
  Pallas kernels: 0 us -> 13.7 us
  between operations: 13.8 us -> 0.19 us
  waiting for transfers between devices: 9.34 us -> 1.14 us
  other arithmetic: 4.1 us -> 0.1 us
    all_gather x1 -> x0, blocking collectives: 25.2 us -> none  [local(): lax.all_gather(row_wire, 'row', axis=0, tiled=True)]
    dot_general x15 -> x0, matrix products: 19.1 us -> none  [the longest x1 4.78 us: local(): jnp.einsum('nlks,lkst->nlt', sources, near_blocks, preferred_element_type...]
    all_to_all x0 -> x2, starting transfers between devices: none -> 18.7 us  [the longest x1 11 us: local(): row_poles = lax.all_to_all(row_wire, 'row', 0, 0, tiled=True)]
    gather x5 -> x0, local copies, waits for them, and re-layouts: 16 us -> none  [the longest x2 12.5 us: local(): ordered = jnp.take(inputs, morton_order, axis=1)]
    pallas_call x0 -> x3, Pallas kernels: none -> 13.7 us  [the longest x1 4.7 us: up_call(): pl.pallas_call(up_kernel, out_shape=(shape((cols, rhs // 2, LANES), F32),...]
    scatter x2 -> x0, local copies, waits for them, and re-layouts: 12.2 us -> none  [local(): return jnp.zeros_like(summed).at[:, morton_order].set(summed)]
    ppermute x6 -> x5, waiting for transfers between devices: 9.3 us -> 0.01 us  [the longest x2 0.01 us: swap(): lax.ppermute(value, ('row', 'col'), pairs + [(b, a) for a, b in pairs])]
    select_n x4 -> x0, other arithmetic: 2.16 us -> none  [the longest x1 2.15 us: local(): ordered = jnp.take(inputs, morton_order, axis=1)]
  transfers between devices with their start and end apart: 7 -> 7, of which waited for: 3 -> 1; matrix products, arithmetic and copies ran while one was open for 11% -> 1% of each run, Pallas kernels for 0% -> 10%
where the time goes in v1:
time: 45.6 us; the launch traced here: 45.3 us
  starting transfers between devices  29.5 us (65%)
  Pallas kernels  13.7 us (30%)
  waiting for transfers between devices  1.14 us (2%)
  local copies, waits for them, and re-layouts  0.69 us (2%)
    all_to_all x1, starting transfers between devices, local(): row_poles = lax.all_to_all(row_wire, 'row', 0, 0, tiled=True)  11 us
    all_to_all x1, starting transfers between devices, local(): everyone = lax.all_to_all(lifted, 'col', 0, 0, tiled=True)  7.72 us
    ppermute x2, starting transfers between devices, swap(): lax.ppermute(value, ('row', 'col'), pairs + [(b, a) for a, b in pairs])  5.82 us
    pallas_call x1, Pallas kernels, up_call(): pl.pallas_call(up_kernel, out_shape=(shape((cols, rhs // 2, LANES), F32),...  4.7 us
    pallas_call x1, Pallas kernels, down_call(): pl.pallas_call(down_kernel, out_shape=jax.ShapeDtypeStruct((rhs, leaf_cou...  4.67 us
    pallas_call x1, Pallas kernels, near_call(): pl.pallas_call(near_kernel, out_shape=jax.ShapeDtypeStruct((leaf_count, r...  4.33 us
    ppermute x1, starting transfers between devices, local(): around = lax.ppermute(first[2 * REACH:], ('row', 'col'), turn)  2.65 us
    ppermute x2, starting transfers between devices, from_peer(): lax.ppermute(value, 'col', [((c + away) % cols, c) for c in range(cols)])  2.34 us
  transfers between devices with their start and end apart: 7, of which 1 were waited for; matrix products, arithmetic and copies ran while one was open for 1% of the time, Pallas kernels for 10%

profile of v1, /device:TPU:1, one launch (start us, length us, event | category | flops | bytes accessed | tf_op | source)
XLA Modules:
  0.0 45.3 jit_solution(13002411482250763697)
XLA Ops:
  0.0 0.1 pad_add_fusion.place
  0.1 4.7 %up.2 = (f32[16,16,128]{2,1,0:T(8,128)}, bf16[16,32,128]{2,1,0:T(8,128)(2,1)S(1)}, bf16[16,32,128]{2,1,0:T(8,128)(2,1)S(1)}, bf16[8,32,128]{2,1,0:T(8,128)(2,1)S...) custom-call(s32[4]{0:T(128)S(1)} %pad_add_fusion.place, bf16[32,4096]{1,0:T(8,128)(2,1)} %x_hbm.1, ...), custom_call_target="tpu_custom_call" | custom-call | flops 4294967296 | bytes 3145728 | tf_op jit(solution)/shard_map/up/pallas_call | solution.py:116
  4.8 0.0 copy-start.1
  4.8 0.0 copy-start.2
  4.8 0.0 copy-start.3
  4.8 0.0 copy-start.4
  4.8 0.0 copy-start.5
  4.9 0.0 copy-start.6
  4.9 7.7 %all-to-all-start = ((f32[16,16,128]{2,1,0:T(8,128)}), f32[16,16,128]{2,1,0:T(8,128)S(1)}, u32[]{:S(2)}, u32[]{:S(2)}) async-start(f32[16,16,128]{2,1,0:T(8,128)} %get-tuple-element.14), calls=%async_computation | async-start | bytes 262144 | tf_op jit(solution)/shard_map/all_to_all | solution.py:309
  12.6 5.8 %collective-permute-start = (bf16[16,32,128]{2,1,0:T(8,128)(2,1)S(1)}, bf16[16,32,128]{2,1,0:T(8,128)(2,1)S(1)}, u32[]{:S(2)}, u32[]{:S(2)}) collective-permute-start(bf16[16,32,128]{2,1,0:T(8,128)(2,1)S(1)} %get-tuple-element.11), channel_id=1, source_target_pairs={{1,2},{3,4},{5,6},{7,8},{9,10},{11,12},{13,14},{15,16},{17,18},{19... | collective-permute-start | bytes 393224 | tf_op jit(solution)/shard_map/ppermute | solution.py:313
  18.4 0.0 collective-permute-start.1
  18.4 1.1 %all-to-all-done = f32[16,16,128]{2,1,0:T(8,128)S(1)} async-done(((f32[16,16,128]{2,1,0:T(8,128)}), f32[16,16,128]{2,1,0:T(8,128)S(1)}, u32[]{:S(2)}, u32[]{:S(2)}) %all-to-all-start) | async-done | bytes 131104 | tf_op jit(solution)/shard_map/all_to_all | solution.py:309
  19.6 0.6 %broadcast_in_dim.2 = bf16[16,16,128]{2,1,0:T(8,128)(2,1)} broadcast(bf16[16,128]{1,0:T(8,128)(2,1)S(1)} %reduce_sum.9), dimensions={1,2} | broadcast | bytes 69632 | tf_op jit(solution)/shard_map/broadcast_in_dim | solution.py:320
  20.2 11.0 %all-to-all-start.1 = ((bf16[16,16,128]{2,1,0:T(8,128)(2,1)}), bf16[16,16,128]{2,1,0:T(8,128)(2,1)S(1)}, u32[]{:S(2)}, u32[]{:S(2)}) async-start(bf16[16,16,128]{2,1,0:T(8,128)(2,1)} %broadcast_in_dim.2), calls=%async_computation.1 | async-start | bytes 131072 | tf_op jit(solution)/shard_map/all_to_all | solution.py:321
  31.2 1.1 %collective-permute-start.4 = (bf16[8,32,128]{2,1,0:T(8,128)(2,1)S(1)}, bf16[8,32,128]{2,1,0:T(8,128)(2,1)S(1)}, u32[]{:S(2)}, u32[]{:S(2)}) collective-permute-start(bf16[8,32,128]{2,1,0:T(8,128)(2,1)S(1)} %get-tuple-element.13), channel_id=1, source_target_pairs={{2,0},{3,1},{4,2},{5,3},{6,4},{7,5},{8,6},{9,7},{10,8},{11,9},{12,... | collective-permute-start | bytes 196616 | tf_op jit(solution)/shard_map/ppermute | solution.py:316
  32.3 1.2 %collective-permute-start.3 = (bf16[8,32,128]{2,1,0:T(8,128)(2,1)S(1)}, bf16[8,32,128]{2,1,0:T(8,128)(2,1)S(1)}, u32[]{:S(2)}, u32[]{:S(2)}) collective-permute-start(bf16[8,32,128]{2,1,0:T(8,128)(2,1)S(1)} %get-tuple-element.13), channel_id=1, source_target_pairs={{8,0},{9,1},{10,2},{11,3},{12,4},{13,5},{14,6},{15,7},{0,8},{1,9},... | collective-permute-start | bytes 196616 | tf_op jit(solution)/shard_map/ppermute | solution.py:316
  33.5 0.0 collective-permute-done.first
  33.5 2.6 %collective-permute-start.2 = (bf16[8,32,128]{2,1,0:T(8,128)(2,1)S(1)}, bf16[8,32,128]{2,1,0:T(8,128)(2,1)S(1)}, u32[]{:S(2)}, u32[]{:S(2)}) collective-permute-start(bf16[8,32,128]{2,1,0:T(8,128)(2,1)S(1)} %slice.4), channel_id=1, source_target_pairs={{16,0},{32,16},{48,32},{64,48},{80,64},{96,80},{112,96},{128,112},... | collective-permute-start | bytes 196616 | tf_op jit(solution)/shard_map/ppermute | solution.py:327
  36.2 0.0 collective-permute-done.1.second
  36.2 4.3 %near.1 = f32[16,32,256]{2,1,0:T(8,128)S(1)} custom-call(s32[4]{0:T(128)S(1)} %pad_add_fusion.place, s32[4,16]{1,0:T(4,128)S(1)} %bitcast.5, bf16[32,32,128]{2,1,0:T(8,128)(2,1)S(1)} %get-tuple-element.16.ordered, bf16[16,32,128]{2,1,0:T(8,128)(2,1)S(1)} %collective-permute-done.first, bf16[16,32,128]{2,1,0:T(8,128)(2,1)S(1)} %collective-permute-done.1.second, ...), custom_call_target="tpu_custom_call" | custom-call | flops 1073741824 | bytes 10485760 | tf_op jit(solution)/shard_map/near/pallas_call | solution.py:178
  40.5 0.0 collective-permute-done.4.p3
  40.5 0.0 collective-permute-done.2.around
  40.5 0.0 all-to-all-done.1.rows
  40.6 4.7 %down.1 = bf16[32,4096]{1,0:T(8,128)(2,1)} custom-call(s32[4]{0:T(128)S(1)} %pad_add_fusion.place, s32[4,16]{1,0:T(4,128)S(1)} %bitcast.8, s32[1,3]{1,0:T(1,128)S(1)} %copy-done.6, bf16[16,32,128]{2,1,0:T(8,128)(2,1)S(1)} %collective-permute-done.first, bf16[16,32,128]{2,1,0:T(8,128)(2,1)S(1)} %collective-permute-done.1.second, ...), custom_call_target="tpu_custom_call" | custom-call | flops 1073741824 | bytes 3145728 | tf_op jit(solution)/shard_map/down/pallas_call | solution.py:267
  (12 shorter events, 0.0 us)
Async XLA Ops:
  0.0 36.2 %copy-start = (s32[16,4]{0,1:T(4,128)S(1)}, s32[16,4]{0,1:T(4,128)}, u32[]{:S(2)}) copy-start(s32[16,4]{0,1:T(4,128)} %param.21) | copy-start | bytes 772
  4.8 35.8 %copy-start.1 = (bf16[16,64,256]{2,1,0:T(8,128)(2,1)S(1)}, bf16[16,64,256]{2,1,0:T(8,128)(2,1)}, u32[]{:S(2)}) copy-start(bf16[16,64,256]{2,1,0:T(8,128)(2,1)} %basis.1) | copy-start | bytes 1572868
  4.8 35.8 %copy-start.2 = (f32[16,64,64]{2,1,0:T(8,128)S(1)}, f32[16,64,64]{2,1,0:T(8,128)}, u32[]{:S(2)}) copy-start(f32[16,64,64]{2,1,0:T(8,128)} %leaf_up.1) | copy-start | bytes 786436
  4.8 35.8 %copy-start.3 = (bf16[1,3,64,64]{3,2,1,0:T(8,128)(2,1)S(1)}, bf16[1,3,64,64]{3,2,1,0:T(8,128)(2,1)}, u32[]{:S(2)}) copy-start(bf16[1,3,64,64]{3,2,1,0:T(8,128)(2,1)} %couple_row.1) | copy-start | bytes 73732
  4.8 35.8 %copy-start.4 = (s32[4096]{0:T(1024)S(1)}, s32[4096]{0:T(1024)}, u32[]{:S(2)}) copy-start(s32[4096]{0:T(1024)} %param.12) | copy-start | bytes 49156
  4.8 35.8 %copy-start.5 = (s32[16,4]{0,1:T(4,128)S(1)}, s32[16,4]{0,1:T(4,128)}, u32[]{:S(2)}) copy-start(s32[16,4]{0,1:T(4,128)} %param.17) | copy-start | bytes 772
  4.9 35.8 %copy-start.6 = (s32[1,3]{1,0:T(1,128)S(1)}, s32[1,3]{1,0:T(1,128)}, u32[]{:S(2)}) copy-start(s32[1,3]{1,0:T(1,128)} %row_lists.1) | copy-start | bytes 40
  4.9 14.7 %all-to-all-start = ((f32[16,16,128]{2,1,0:T(8,128)}), f32[16,16,128]{2,1,0:T(8,128)S(1)}, u32[]{:S(2)}, u32[]{:S(2)}) async-start(f32[16,16,128]{2,1,0:T(8,128)} %get-tuple-element.14), calls=%async_computation | async-start | bytes 262144 | tf_op jit(solution)/shard_map/all_to_all | solution.py:309
  12.6 20.9 %collective-permute-start = (bf16[16,32,128]{2,1,0:T(8,128)(2,1)S(1)}, bf16[16,32,128]{2,1,0:T(8,128)(2,1)S(1)}, u32[]{:S(2)}, u32[]{:S(2)}) collective-permute-start(bf16[16,32,128]{2,1,0:T(8,128)(2,1)S(1)} %get-tuple-element.11), channel_id=1, source_target_pairs={{1,2},{3,4},{5,6},{7,8},{9,10},{11,12},{13,14},{15,16},{17,18},{19... | collective-permute-start | bytes 393224 | tf_op jit(solution)/shard_map/ppermute | solution.py:313
  18.4 17.7 %collective-permute-start.1 = (bf16[16,32,128]{2,1,0:T(8,128)(2,1)S(1)}, bf16[16,32,128]{2,1,0:T(8,128)(2,1)S(1)}, u32[]{:S(2)}, u32[]{:S(2)}) collective-permute-start(bf16[16,32,128]{2,1,0:T(8,128)(2,1)S(1)} %get-tuple-element.12), channel_id=1, source_target_pairs={{0,1},{2,3},{4,5},{6,7},{8,9},{10,11},{12,13},{14,15},{16,17},{18,... | collective-permute-start | bytes 393224 | tf_op jit(solution)/shard_map/ppermute | solution.py:313
  20.2 20.4 %all-to-all-start.1 = ((bf16[16,16,128]{2,1,0:T(8,128)(2,1)}), bf16[16,16,128]{2,1,0:T(8,128)(2,1)S(1)}, u32[]{:S(2)}, u32[]{:S(2)}) async-start(bf16[16,16,128]{2,1,0:T(8,128)(2,1)} %broadcast_in_dim.2), calls=%async_computation.1 | async-start | bytes 131072 | tf_op jit(solution)/shard_map/all_to_all | solution.py:321
  31.2 9.4 %collective-permute-start.4 = (bf16[8,32,128]{2,1,0:T(8,128)(2,1)S(1)}, bf16[8,32,128]{2,1,0:T(8,128)(2,1)S(1)}, u32[]{:S(2)}, u32[]{:S(2)}) collective-permute-start(bf16[8,32,128]{2,1,0:T(8,128)(2,1)S(1)} %get-tuple-element.13), channel_id=1, source_target_pairs={{2,0},{3,1},{4,2},{5,3},{6,4},{7,5},{8,6},{9,7},{10,8},{11,9},{12,... | collective-permute-start | bytes 196616 | tf_op jit(solution)/shard_map/ppermute | solution.py:316
  32.3 8.2 %collective-permute-start.3 = (bf16[8,32,128]{2,1,0:T(8,128)(2,1)S(1)}, bf16[8,32,128]{2,1,0:T(8,128)(2,1)S(1)}, u32[]{:S(2)}, u32[]{:S(2)}) collective-permute-start(bf16[8,32,128]{2,1,0:T(8,128)(2,1)S(1)} %get-tuple-element.13), channel_id=1, source_target_pairs={{8,0},{9,1},{10,2},{11,3},{12,4},{13,5},{14,6},{15,7},{0,8},{1,9},... | collective-permute-start | bytes 196616 | tf_op jit(solution)/shard_map/ppermute | solution.py:316
  33.5 7.0 %collective-permute-start.2 = (bf16[8,32,128]{2,1,0:T(8,128)(2,1)S(1)}, bf16[8,32,128]{2,1,0:T(8,128)(2,1)S(1)}, u32[]{:S(2)}, u32[]{:S(2)}) collective-permute-start(bf16[8,32,128]{2,1,0:T(8,128)(2,1)S(1)} %slice.4), channel_id=1, source_target_pairs={{16,0},{32,16},{48,32},{64,48},{80,64},{96,80},{112,96},{128,112},... | collective-permute-start | bytes 196616 | tf_op jit(solution)/shard_map/ppermute | solution.py:327

commit v2 on v1

--- a/solution.py
+++ b/solution.py
@@ -14,7 +14,6 @@
 ANY = pl.BlockSpec(memory_space=pl.ANY)
 LANES = 128
 GROUP = 2
-AHEAD = 8
 
 
 def in_hbm(value):
@@ -32,6 +31,27 @@
 def halves(value):
     high = value.astype(BF)
     return high, (value - high.astype(F32)).astype(BF)
+
+
+def chained(steps):
+    wholes = [steps[h] for h in range(steps.shape[0])]
+    while len(wholes) > 1:
+        joined = [
+            jnp.dot(a, b, precision=HIGHEST, preferred_element_type=F32)
+            for a, b in zip(wholes[::2], wholes[1::2])
+        ]
+        wholes = joined + wholes[2 * len(joined) :]
+    return wholes[0]
+
+
+def fetch_steps(up, steps, sems, col):
+    depth = steps.shape[0]
+    cols = 1 << depth
+    copies = []
+    for h in range(depth):
+        node = 2 * cols - 2 * (cols >> h) + (col >> h)
+        copies.append(pltpu.make_async_copy(up.at[0, node], steps.at[h], sems.at[h]))
+    return copies
 
 
 def one_hot(low, size):
@@ -41,12 +61,11 @@
 
 
 def up_kernel(
-    place, x_hbm, order_hbm, basis_hbm, leaf_up_hbm, up, lifted, first_out, second_out, poles, ordered, chain,
-    x, order, basis, leaf_up, steps, sems,
+    place, x_hbm, order_hbm, basis_hbm, leaf_up_hbm, up, lifted, first_out, second_out, poles, ordered,
+    x, order, basis, leaf_up, steps, sems, step_sems,
 ):
     leaf_count, rank, points = basis.shape
     rhs = x.shape[0]
-    depth = steps.shape[0]
     half = leaf_count // 2
     edge = 2 * REACH
     col, cols = place[0], lifted.shape[0]
@@ -54,19 +73,14 @@
         pltpu.make_async_copy(order_hbm, order, sems.at[0]),
         pltpu.make_async_copy(x_hbm, x, sems.at[1]),
     ]
-    for h in range(depth):
-        node = 2 * cols - 2 * (cols >> h) + (col >> h)
-        first.append(pltpu.make_async_copy(up.at[0, node], steps.at[h], sems.at[4 + h]))
+    first += fetch_steps(up, steps, step_sems, col)
     second = [pltpu.make_async_copy(basis_hbm, basis, sems.at[2])]
     third = [pltpu.make_async_copy(leaf_up_hbm, leaf_up, sems.at[3])]
     for copy in first + second + third:
         copy.start()
     for copy in first:
         copy.wait()
-    whole = steps[0]
-    for h in range(1, depth):
-        whole = jnp.dot(whole, steps[h], precision=HIGHEST, preferred_element_type=F32)
-    chain[...] = whole
+    whole = chained(steps)
     slabs = jnp.concatenate(
         [x[:, a * points : (a + 1) * points] for a in range(leaf_count)], axis=0
     )
@@ -85,8 +99,20 @@
         leaves.append(leaf)
     for copy in second:
         copy.wait()
-    moments = [mm_t(leaves[i], basis[i]).astype(BF) for i in range(leaf_count)]
-    pairs = [jnp.concatenate(moments[i : i + 2], axis=1) for i in range(0, leaf_count, 2)]
+    group = points // rank
+    lane = lax.broadcasted_iota(jnp.int32, (rhs, points), 1) // rank
+    quads = []
+    for i in range(0, leaf_count, group):
+        crossed = mm_t(
+            jnp.concatenate(leaves[i : i + group], axis=0),
+            basis[i : i + group].reshape(group * rank, points),
+        )
+        quad = crossed[:rhs]
+        for j in range(1, group):
+            quad = jnp.where(lane == j, crossed[j * rhs : (j + 1) * rhs], quad)
+        quads.append(quad.astype(BF))
+    every = jnp.concatenate(quads, axis=1)
+    pairs = [every[:, q * LANES : (q + 1) * LANES] for q in range(half)]
     for q in range(half):
         poles[q] = pairs[q]
         first_out[edge + q] = pairs[q]
@@ -94,7 +120,6 @@
     for copy in third:
         copy.wait()
     up_high, up_low = halves(leaf_up[...].reshape(leaf_count * rank, rank))
-    every = jnp.concatenate(pairs, axis=1)
     top = mm(every, up_high) + mm(every, up_low)
     top = jnp.dot(top, whole, precision=HIGHEST, preferred_element_type=F32)
     packed = jnp.concatenate([top[: rhs // 2], top[rhs // 2 :]], axis=1)
@@ -121,17 +146,17 @@
             sent,
             shape((half, rhs, LANES), BF),
             shape((2 * leaf_count, rhs, LANES), BF),
-            shape((rank, rank), F32),
         ),
         in_specs=[SMEM] + [ANY] * 5,
-        out_specs=(VMEM,) * 6,
+        out_specs=(VMEM,) * 5,
         scratch_shapes=[
             pltpu.VMEM(inputs.shape, BF),
             pltpu.VMEM(order.shape, order.dtype),
             pltpu.VMEM(basis.shape, BF),
             pltpu.VMEM(leaf_up.shape, F32),
             pltpu.VMEM((depth, rank, rank), F32),
-            pltpu.SemaphoreType.DMA((4 + depth,)),
+            pltpu.SemaphoreType.DMA((4,)),
+            pltpu.SemaphoreType.DMA((depth,)),
         ],
         compiler_params=pltpu.CompilerParams(vmem_limit_bytes=24 << 20),
         cost_estimate=pl.CostEstimate(flops=1 << 32, bytes_accessed=3 << 20, transcendentals=0),
@@ -139,7 +164,9 @@
     )(place, in_hbm(inputs), in_hbm(order), in_hbm(basis), in_hbm(leaf_up), in_hbm(up_transfer))
 
 
-def near_kernel(place, offsets, ordered, first, second, blocks_hbm, near, extended, blocks, sems):
+def near_kernel(
+    place, offsets, ordered, first, second, blocks_hbm, up, near, extended, blocks, steps, sems, step_sems
+):
     leaf_count, count, points, _ = blocks.shape
     col, row, rows, cols = place[0], place[1], place[2], place[3]
     edge = 2 * REACH
@@ -150,7 +177,8 @@
         )
         for i in range(0, leaf_count, group)
     ]
-    for copy in fetched[:AHEAD]:
+    small = fetch_steps(up, steps, step_sems, col)
+    for copy in small + fetched:
         copy.start()
     odd = (col & 1) == 1
     lowest = (col == 0) & (row == 0)
@@ -163,8 +191,13 @@
     for i in range(leaf_count):
         if i % group == 0:
             fetched[i // group].wait()
-            if i // group + AHEAD < len(fetched):
-                fetched[i // group + AHEAD].start()
+        if i == leaf_count - 2:
+            for copy in small:
+                copy.wait()
+            whole = chained(steps)
+            half = whole.shape[0] // 2
+            near[leaf_count, :half, : 2 * half] = whole[:half]
+            near[leaf_count, :half, LANES : LANES + 2 * half] = whole[half:]
         parts = []
         for k in range(count):
             at = 2 * (i + REACH + offsets[k, i])
@@ -172,49 +205,43 @@
         near[i] = mm(jnp.concatenate(parts, axis=1), blocks[i].reshape(count * points, points))
 
 
-def near_call(place, offsets, ordered, first, second, near_blocks):
+def near_call(place, offsets, ordered, first, second, near_blocks, up_transfer, cols):
     leaf_count, _, points, _ = near_blocks.shape
+    rank = up_transfer.shape[-1]
+    depth = cols.bit_length() - 1
     rhs = ordered.shape[1]
     return pl.pallas_call(
         near_kernel,
-        out_shape=jax.ShapeDtypeStruct((leaf_count, rhs, points), F32),
-        in_specs=[SMEM, SMEM] + [VMEM] * 3 + [ANY],
+        out_shape=jax.ShapeDtypeStruct((leaf_count + 1, rhs, points), F32),
+        in_specs=[SMEM, SMEM] + [VMEM] * 3 + [ANY] * 2,
         out_specs=VMEM,
         scratch_shapes=[
             pltpu.VMEM((2 * leaf_count + 4 * REACH, rhs, LANES), BF),
             pltpu.VMEM(near_blocks.shape, BF),
+            pltpu.VMEM((depth, rank, rank), F32),
             pltpu.SemaphoreType.DMA((leaf_count // GROUP,)),
+            pltpu.SemaphoreType.DMA((depth,)),
         ],
         compiler_params=pltpu.CompilerParams(vmem_limit_bytes=24 << 20),
-        cost_estimate=pl.CostEstimate(flops=1 << 30, bytes_accessed=10 << 20, transcendentals=0),
+        cost_estimate=pl.CostEstimate(flops=1 << 30, bytes_accessed=1 << 20, transcendentals=0),
         name="near",
-    )(place, offsets, ordered, first, second, in_hbm(near_blocks))
+    )(place, offsets, ordered, first, second, in_hbm(near_blocks), in_hbm(up_transfer))
 
 
 def down_kernel(
-    place, lists, row_lists, first, second, around, p1, p3, couple_hbm, rows, couple_row, chain, leaf_up,
-    basis, near, order, out, poles, couple, spread, marks, sem,
+    place, lists, row_lists, first, second, around, p1, p3, couple, rows, couple_row, leaf_up,
+    basis, near, order, out, poles, spread, marks,
 ):
     leaf_count, rank, points = basis.shape
     rhs = near.shape[1]
     slots = couple.shape[1]
     edge = 2 * REACH
     col, cols = place[0], place[3]
-    fetched = pltpu.make_async_copy(couple_hbm, couple, sem)
-    fetched.start()
     odd = (col & 1) == 1
-    poles[0] = jnp.where(odd, second[edge:], first[edge:])
-    poles[2] = jnp.where(odd, first[edge:], second[edge:])
+    poles[0] = jnp.where(col == 0, around[...], jnp.where(odd, second[edge:], first[edge:]))
     poles[1] = p1[...]
+    poles[2] = jnp.where(col == cols - 1, around[...], jnp.where(odd, first[edge:], second[edge:]))
     poles[3] = p3[...]
-
-    @pl.when(col == 0)
-    def _():
-        poles[0] = around[...]
-
-    @pl.when(col == cols - 1)
-    def _():
-        poles[2] = around[...]
 
     for i in range(leaf_count):
         where = order[:, i * points : (i + 1) * points]
@@ -234,17 +261,29 @@
     local_row = mm(
         jnp.concatenate(sources, axis=1), couple_row[0].reshape(len(sources) * rank, rank)
     )
-    fetched.wait()
     sides = [mm(joined[i], couple[i].reshape(slots * rank, rank)) for i in range(leaf_count)]
+    half = rank // 2
+    whole = jnp.concatenate(
+        [near[leaf_count, :half, :rank], near[leaf_count, :half, LANES : LANES + rank]], axis=0
+    )
     downward = lax.dot_general(
-        local_row, chain[...], (((1,), (1,)), ((), ())), precision=HIGHEST, preferred_element_type=F32
+        local_row, whole, (((1,), (1,)), ((), ())), precision=HIGHEST, preferred_element_type=F32
     )
     down_high, down_low = halves(downward)
     up_high, up_low = halves(leaf_up[...].reshape(leaf_count * rank, rank))
     both = mm_t(jnp.concatenate([down_high, down_low], axis=0), up_high)
     pushed = both[:rhs] + both[rhs:] + mm_t(down_high, up_low)
     leaf_local = (jnp.concatenate(sides, axis=1) + pushed).astype(BF)
-    fars = [mm(leaf_local[:, i * rank : (i + 1) * rank], basis[i]) for i in range(leaf_count)]
+    group = points // rank
+    lane = lax.broadcasted_iota(jnp.int32, (rhs, points), 1) // rank
+    fars = []
+    for i in range(0, leaf_count, group):
+        several = leaf_local[:, i * rank : (i + group) * rank]
+        apart = jnp.concatenate(
+            [jnp.where(lane == j, several, jnp.zeros_like(several)) for j in range(group)], axis=0
+        )
+        together = mm(apart, basis[i : i + group].reshape(group * rank, points))
+        fars += [together[j * rhs : (j + 1) * rhs] for j in range(group)]
     for i in range(leaf_count):
         high = (order[:, i * points : (i + 1) * points] // points).astype(BF)
         high = jnp.broadcast_to(high, (rhs, points))
@@ -259,7 +298,7 @@
 
 
 def down_call(
-    place, lists, row_lists, first, second, around, p1, p3, couple, row_poles, couple_row, chain, leaf_up,
+    place, lists, row_lists, first, second, around, p1, p3, couple, row_poles, couple_row, leaf_up,
     basis, near, order,
 ):
     leaf_count, rank, points = basis.shape
@@ -267,21 +306,19 @@
     return pl.pallas_call(
         down_kernel,
         out_shape=jax.ShapeDtypeStruct((rhs, leaf_count * points), BF),
-        in_specs=[SMEM] * 3 + [VMEM] * 5 + [ANY] + [VMEM] * 7,
+        in_specs=[SMEM] * 3 + [VMEM] * 12,
         out_specs=VMEM,
         scratch_shapes=[
             pltpu.VMEM((couple.shape[1], *p1.shape), BF),
-            pltpu.VMEM(couple.shape, BF),
             pltpu.VMEM((leaf_count * rhs, leaf_count * points), BF),
             pltpu.VMEM((points, leaf_count * points), BF),
-            pltpu.SemaphoreType.DMA,
         ],
         compiler_params=pltpu.CompilerParams(vmem_limit_bytes=24 << 20),
-        cost_estimate=pl.CostEstimate(flops=1 << 30, bytes_accessed=3 << 20, transcendentals=0),
+        cost_estimate=pl.CostEstimate(flops=1 << 28, bytes_accessed=3 << 20, transcendentals=0),
         name="down",
     )(
-        place, lists, row_lists, first, second, around, p1, p3, in_hbm(couple), row_poles, couple_row,
-        chain, leaf_up, basis, near, order,
+        place, lists, row_lists, first, second, around, p1, p3, couple, row_poles, couple_row,
+        leaf_up, basis, near, order,
     )
 
 
@@ -303,7 +340,7 @@
     count = rows * cols
     place = jnp.stack([lax.axis_index("col"), lax.axis_index("row"), rows, cols]).astype(jnp.int32)
     order = morton_order.reshape(1, -1)
-    lifted, first, second, poles, ordered, chain = up_call(
+    lifted, first, second, poles, ordered = up_call(
         place, inputs, order, basis, leaf_up, up_transfer, cols
     )
     everyone = lax.all_to_all(lifted, "col", 0, 0, tiled=True)
@@ -322,13 +359,16 @@
     second = swap(second, 0)
     p1 = from_peer(poles, cols // 2)
     p3 = from_peer(poles, 2)
-    turn = [(((r + 1) % rows) * cols, r * cols) for r in range(rows)]
-    turn += [(r * cols + cols - 1, ((r + 1) % rows) * cols + cols - 1) for r in range(rows)]
+    down_rows = [(((r + 1) % rows) * cols + c, r * cols + c) for r in range(rows) for c in range(cols // 2)]
+    up_rows = [(r * cols + c, ((r + 1) % rows) * cols + c) for r in range(rows) for c in range(cols // 2, cols)]
+    turn = down_rows + up_rows
     around = lax.ppermute(first[2 * REACH :], ("row", "col"), turn)
-    near = near_call(place, near_offsets.T, ordered, first, second, near_blocks)
+    near = near_call(
+        place, near_offsets.T, ordered, first, second, near_blocks, up_transfer, cols
+    )
     return down_call(
         place, leaf_lists.T, row_lists, first, second, around, p1, p3, couple_leaf, row_poles, couple_row,
-        chain, leaf_up, basis, near, order,
+        leaf_up, basis, near, order,
     )
 
 

time: 45.6 us -> 43.8 us (0.961)
  the two profiles are of different devices: /device:TPU:1 before, /device:TPU:7 now
where the time goes in v2:
time: 43.8 us; the launch traced here: 43.5 us
  starting transfers between devices  27.1 us (62%)
  Pallas kernels  12.9 us (29%)
  waiting for transfers between devices  2.49 us (6%)
  local copies, waits for them, and re-layouts  0.69 us (2%)
    all_to_all x1, starting transfers between devices, local(): row_poles = lax.all_to_all(row_wire, 'row', 0, 0, tiled=True)  10.8 us
    all_to_all x1, starting transfers between devices, local(): everyone = lax.all_to_all(lifted, 'col', 0, 0, tiled=True)  7.01 us
    pallas_call x1, Pallas kernels, near_call(): pl.pallas_call(near_kernel, out_shape=jax.ShapeDtypeStruct((leaf_count +...  4.66 us
    pallas_call x1, Pallas kernels, up_call(): pl.pallas_call(up_kernel, out_shape=(shape((cols, rhs // 2, LANES), F32),...  4.62 us
    ppermute x2, starting transfers between devices, from_peer(): lax.ppermute(value, 'col', [((c + away) % cols, c) for c in range(cols)])  4.38 us
    pallas_call x1, Pallas kernels, down_call(): pl.pallas_call(down_kernel, out_shape=jax.ShapeDtypeStruct((rhs, leaf_cou...  3.65 us
    ppermute x2, starting transfers between devices, swap(): lax.ppermute(value, ('row', 'col'), pairs + [(b, a) for a, b in pairs])  2.69 us
    all_to_all x1, waiting for transfers between devices, local(): everyone = lax.all_to_all(lifted, 'col', 0, 0, tiled=True)  2.47 us
  transfers between devices with their start and end apart: 7, of which 1 were waited for; matrix products, arithmetic and copies ran while one was open for 2% of the time, Pallas kernels for 11%

profile of v2, /device:TPU:7, one launch (start us, length us, event | category | flops | bytes accessed | tf_op | source)
XLA Modules:
  0.0 43.5 jit_solution(11116594117616270690)
XLA Ops:
  0.0 0.1 pad_add_fusion.place
  0.1 4.6 %up.3 = (f32[16,16,128]{2,1,0:T(8,128)}, bf16[16,32,128]{2,1,0:T(8,128)(2,1)S(1)}, bf16[16,32,128]{2,1,0:T(8,128)(2,1)S(1)}, bf16[8,32,128]{2,1,0:T(8,128)(2,1)}, bf16[32,32,128]{2,1,0:T(8,128)(2,1)S(1)}) custom-call(s32[4]{0:T(128)S(1)} %pad_add_fusion.place, bf16[32,4096]{1,0:T(8,128)(2,1)} %x_hbm.1, s32[1,4096]{1,0:T(1,128)} %bitcast.5, ...), custom_call_target="tpu_custom_call" | custom-call | flops 4294967296 | bytes 3145728 | tf_op jit(solution)/shard_map/up/pallas_call | solution.py:141
  4.7 0.0 copy-start
  4.7 0.0 copy-start.1
  4.7 0.0 copy-start.2
  4.8 0.0 copy-start.3
  4.8 0.0 copy-start.4
  4.8 0.0 copy-start.6
  4.8 0.0 copy-start.7
  4.8 7.0 %all-to-all-start = ((f32[16,16,128]{2,1,0:T(8,128)}), f32[16,16,128]{2,1,0:T(8,128)S(1)}, u32[]{:S(2)}, u32[]{:S(2)}) async-start(f32[16,16,128]{2,1,0:T(8,128)} %get-tuple-element.13), calls=%async_computation | async-start | bytes 262144 | tf_op jit(solution)/shard_map/all_to_all | solution.py:346
  11.8 2.7 %collective-permute-start = (bf16[16,32,128]{2,1,0:T(8,128)(2,1)S(1)}, bf16[16,32,128]{2,1,0:T(8,128)(2,1)S(1)}, u32[]{:S(2)}, u32[]{:S(2)}) collective-permute-start(bf16[16,32,128]{2,1,0:T(8,128)(2,1)S(1)} %get-tuple-element.10), channel_id=1, source_target_pairs={{1,2},{3,4},{5,6},{7,8},{9,10},{11,12},{13,14},{15,16},{17,18},{19... | collective-permute-start | bytes 393224 | tf_op jit(solution)/shard_map/ppermute | solution.py:350
  14.5 0.0 collective-permute-start.1
  14.5 2.5 %all-to-all-done = f32[16,16,128]{2,1,0:T(8,128)S(1)} async-done(((f32[16,16,128]{2,1,0:T(8,128)}), f32[16,16,128]{2,1,0:T(8,128)S(1)}, u32[]{:S(2)}, u32[]{:S(2)}) %all-to-all-start) | async-done | bytes 131104 | tf_op jit(solution)/shard_map/all_to_all | solution.py:346
  17.0 0.6 %broadcast_in_dim.2 = bf16[16,16,128]{2,1,0:T(8,128)(2,1)} broadcast(bf16[16,128]{1,0:T(8,128)(2,1)S(1)} %reduce_sum.9), dimensions={1,2} | broadcast | bytes 69632 | tf_op jit(solution)/shard_map/broadcast_in_dim | solution.py:357
  17.6 10.8 %all-to-all-start.1 = ((bf16[16,16,128]{2,1,0:T(8,128)(2,1)}), bf16[16,16,128]{2,1,0:T(8,128)(2,1)S(1)}, u32[]{:S(2)}, u32[]{:S(2)}) async-start(bf16[16,16,128]{2,1,0:T(8,128)(2,1)} %broadcast_in_dim.2), calls=%async_computation.1 | async-start | bytes 131072 | tf_op jit(solution)/shard_map/all_to_all | solution.py:358
  28.4 1.0 %collective-permute-start.4 = (bf16[8,32,128]{2,1,0:T(8,128)(2,1)}, bf16[8,32,128]{2,1,0:T(8,128)(2,1)S(1)}, u32[]{:S(2)}, u32[]{:S(2)}) collective-permute-start(bf16[8,32,128]{2,1,0:T(8,128)(2,1)} %get-tuple-element.12), channel_id=1, source_target_pairs={{2,0},{3,1},{4,2},{5,3},{6,4},{7,5},{8,6},{9,7},{10,8},{11,9},{12,... | collective-permute-start | bytes 196616 | tf_op jit(solution)/shard_map/ppermute | solution.py:353
  29.4 3.4 %collective-permute-start.3 = (bf16[8,32,128]{2,1,0:T(8,128)(2,1)}, bf16[8,32,128]{2,1,0:T(8,128)(2,1)S(1)}, u32[]{:S(2)}, u32[]{:S(2)}) collective-permute-start(bf16[8,32,128]{2,1,0:T(8,128)(2,1)} %get-tuple-element.12), channel_id=1, source_target_pairs={{8,0},{9,1},{10,2},{11,3},{12,4},{13,5},{14,6},{15,7},{0,8},{1,9},... | collective-permute-start | bytes 196616 | tf_op jit(solution)/shard_map/ppermute | solution.py:353
  32.8 0.0 collective-permute-done.first
  32.8 2.3 %collective-permute-start.2 = (bf16[8,32,128]{2,1,0:T(8,128)(2,1)S(1)}, bf16[8,32,128]{2,1,0:T(8,128)(2,1)S(1)}, u32[]{:S(2)}, u32[]{:S(2)}) collective-permute-start(bf16[8,32,128]{2,1,0:T(8,128)(2,1)S(1)} %slice.4), channel_id=1, source_target_pairs={{16,0},{17,1},{18,2},{19,3},{20,4},{21,5},{22,6},{23,7},{32,16},{3... | collective-permute-start | bytes 196616 | tf_op jit(solution)/shard_map/ppermute | solution.py:365
  35.1 0.0 collective-permute-done.1.second
  35.1 4.7 %near.1 = f32[17,32,256]{2,1,0:T(8,128)S(1)} custom-call(s32[4]{0:T(128)S(1)} %pad_add_fusion.place, s32[4,16]{1,0:T(4,128)S(1)} %bitcast.7, bf16[32,32,128]{2,1,0:T(8,128)(2,1)S(1)} %get-tuple-element.14.ordered, bf16[16,32,128]{2,1,0:T(8,128)(2,1)S(1)} %collective-permute-done.first, bf16[16,32,128]{2,1,0:T(8,128)(2,1)S(1)} %collective-permute-done.1.second, ...), custom_call_target="tpu_custom_call" | custom-call | flops 1073741824 | bytes 1048576 | tf_op jit(solution)/shard_map/near/pallas_call | solution.py:213
  39.8 0.0 collective-permute-done.2.around
  39.8 0.0 all-to-all-done.1.rows
  39.8 3.6 %down.1 = bf16[32,4096]{1,0:T(8,128)(2,1)} custom-call(s32[4]{0:T(128)S(1)} %pad_add_fusion.place, s32[4,16]{1,0:T(4,128)S(1)} %bitcast.8, s32[1,3]{1,0:T(1,128)S(1)} %copy-done.7, bf16[16,32,128]{2,1,0:T(8,128)(2,1)S(1)} %collective-permute-done.first, bf16[16,32,128]{2,1,0:T(8,128)(2,1)S(1)} %collective-permute-done.1.second, ...), custom_call_target="tpu_custom_call" | custom-call | flops 268435456 | bytes 3145728 | tf_op jit(solution)/shard_map/down/pallas_call | solution.py:306
  (14 shorter events, 0.1 us)
Async XLA Ops:
  0.0 35.1 %copy-start.5 = (s32[16,4]{0,1:T(4,128)S(1)}, s32[16,4]{0,1:T(4,128)}, u32[]{:S(2)}) copy-start(s32[16,4]{0,1:T(4,128)} %param.21) | copy-start | bytes 772
  4.7 35.1 %copy-start = (bf16[16,4,64,64]{3,2,1,0:T(8,128)(2,1)S(1)}, bf16[16,4,64,64]{3,2,1,0:T(8,128)(2,1)}, u32[]{:S(2)}) copy-start(bf16[16,4,64,64]{3,2,1,0:T(8,128)(2,1)} %couple.1) | copy-start | bytes 1572868
  4.7 35.1 %copy-start.1 = (bf16[16,64,256]{2,1,0:T(8,128)(2,1)S(1)}, bf16[16,64,256]{2,1,0:T(8,128)(2,1)}, u32[]{:S(2)}) copy-start(bf16[16,64,256]{2,1,0:T(8,128)(2,1)} %basis.1) | copy-start | bytes 1572868
  4.7 35.1 %copy-start.2 = (f32[16,64,64]{2,1,0:T(8,128)S(1)}, f32[16,64,64]{2,1,0:T(8,128)}, u32[]{:S(2)}) copy-start(f32[16,64,64]{2,1,0:T(8,128)} %leaf_up.1) | copy-start | bytes 786436
  4.8 35.1 %copy-start.3 = (bf16[1,3,64,64]{3,2,1,0:T(8,128)(2,1)S(1)}, bf16[1,3,64,64]{3,2,1,0:T(8,128)(2,1)}, u32[]{:S(2)}) copy-start(bf16[1,3,64,64]{3,2,1,0:T(8,128)(2,1)} %couple_row.1) | copy-start | bytes 73732
  4.8 35.1 %copy-start.4 = (s32[4096]{0:T(1024)S(1)}, s32[4096]{0:T(1024)}, u32[]{:S(2)}) copy-start(s32[4096]{0:T(1024)} %param.12) | copy-start | bytes 49156
  4.8 35.1 %copy-start.6 = (s32[16,4]{0,1:T(4,128)S(1)}, s32[16,4]{0,1:T(4,128)}, u32[]{:S(2)}) copy-start(s32[16,4]{0,1:T(4,128)} %param.17) | copy-start | bytes 772
  4.8 35.0 %copy-start.7 = (s32[1,3]{1,0:T(1,128)S(1)}, s32[1,3]{1,0:T(1,128)}, u32[]{:S(2)}) copy-start(s32[1,3]{1,0:T(1,128)} %row_lists.1) | copy-start | bytes 40
  4.8 12.2 %all-to-all-start = ((f32[16,16,128]{2,1,0:T(8,128)}), f32[16,16,128]{2,1,0:T(8,128)S(1)}, u32[]{:S(2)}, u32[]{:S(2)}) async-start(f32[16,16,128]{2,1,0:T(8,128)} %get-tuple-element.13), calls=%async_computation | async-start | bytes 262144 | tf_op jit(solution)/shard_map/all_to_all | solution.py:346
  11.8 21.0 %collective-permute-start = (bf16[16,32,128]{2,1,0:T(8,128)(2,1)S(1)}, bf16[16,32,128]{2,1,0:T(8,128)(2,1)S(1)}, u32[]{:S(2)}, u32[]{:S(2)}) collective-permute-start(bf16[16,32,128]{2,1,0:T(8,128)(2,1)S(1)} %get-tuple-element.10), channel_id=1, source_target_pairs={{1,2},{3,4},{5,6},{7,8},{9,10},{11,12},{13,14},{15,16},{17,18},{19... | collective-permute-start | bytes 393224 | tf_op jit(solution)/shard_map/ppermute | solution.py:350
  14.5 20.6 %collective-permute-start.1 = (bf16[16,32,128]{2,1,0:T(8,128)(2,1)S(1)}, bf16[16,32,128]{2,1,0:T(8,128)(2,1)S(1)}, u32[]{:S(2)}, u32[]{:S(2)}) collective-permute-start(bf16[16,32,128]{2,1,0:T(8,128)(2,1)S(1)} %get-tuple-element.11), channel_id=1, source_target_pairs={{0,1},{2,3},{4,5},{6,7},{8,9},{10,11},{12,13},{14,15},{16,17},{18,... | collective-permute-start | bytes 393224 | tf_op jit(solution)/shard_map/ppermute | solution.py:350
  17.6 22.1 %all-to-all-start.1 = ((bf16[16,16,128]{2,1,0:T(8,128)(2,1)}), bf16[16,16,128]{2,1,0:T(8,128)(2,1)S(1)}, u32[]{:S(2)}, u32[]{:S(2)}) async-start(bf16[16,16,128]{2,1,0:T(8,128)(2,1)} %broadcast_in_dim.2), calls=%async_computation.1 | async-start | bytes 131072 | tf_op jit(solution)/shard_map/all_to_all | solution.py:358
  28.4 11.3 %collective-permute-start.4 = (bf16[8,32,128]{2,1,0:T(8,128)(2,1)}, bf16[8,32,128]{2,1,0:T(8,128)(2,1)S(1)}, u32[]{:S(2)}, u32[]{:S(2)}) collective-permute-start(bf16[8,32,128]{2,1,0:T(8,128)(2,1)} %get-tuple-element.12), channel_id=1, source_target_pairs={{2,0},{3,1},{4,2},{5,3},{6,4},{7,5},{8,6},{9,7},{10,8},{11,9},{12,... | collective-permute-start | bytes 196616 | tf_op jit(solution)/shard_map/ppermute | solution.py:353
  29.4 10.4 %collective-permute-start.3 = (bf16[8,32,128]{2,1,0:T(8,128)(2,1)}, bf16[8,32,128]{2,1,0:T(8,128)(2,1)S(1)}, u32[]{:S(2)}, u32[]{:S(2)}) collective-permute-start(bf16[8,32,128]{2,1,0:T(8,128)(2,1)} %get-tuple-element.12), channel_id=1, source_target_pairs={{8,0},{9,1},{10,2},{11,3},{12,4},{13,5},{14,6},{15,7},{0,8},{1,9},... | collective-permute-start | bytes 196616 | tf_op jit(solution)/shard_map/ppermute | solution.py:353
  32.8 7.0 %collective-permute-start.2 = (bf16[8,32,128]{2,1,0:T(8,128)(2,1)S(1)}, bf16[8,32,128]{2,1,0:T(8,128)(2,1)S(1)}, u32[]{:S(2)}, u32[]{:S(2)}) collective-permute-start(bf16[8,32,128]{2,1,0:T(8,128)(2,1)S(1)} %slice.4), channel_id=1, source_target_pairs={{16,0},{17,1},{18,2},{19,3},{20,4},{21,5},{22,6},{23,7},{32,16},{3... | collective-permute-start | bytes 196616 | tf_op jit(solution)/shard_map/ppermute | solution.py:365

commit v3 on v2

--- a/solution.py
+++ b/solution.py
@@ -164,11 +164,30 @@
     )(place, in_hbm(inputs), in_hbm(order), in_hbm(basis), in_hbm(leaf_up), in_hbm(up_transfer))
 
 
+def ends_kernel(place, ends):
+    lowest = (place[0] == 0) & (place[1] == 0)
+    highest = (place[0] == place[3] - 1) & (place[1] == place[2] - 1)
+    one = jnp.ones(ends.shape[1:], BF)
+    ends[0] = jnp.where(lowest, jnp.zeros_like(one), one)
+    ends[1] = jnp.where(highest, jnp.zeros_like(one), one)
+
+
+def ends_call(place, rhs):
+    return pl.pallas_call(
+        ends_kernel,
+        out_shape=jax.ShapeDtypeStruct((2, rhs, LANES), BF),
+        in_specs=[SMEM],
+        out_specs=VMEM,
+        cost_estimate=pl.CostEstimate(flops=1 << 31, bytes_accessed=1 << 14, transcendentals=0),
+        name="ends",
+    )(place)
+
+
 def near_kernel(
-    place, offsets, ordered, first, second, blocks_hbm, up, near, extended, blocks, steps, sems, step_sems
+    place, offsets, ends, ordered, first, second, blocks_hbm, up, near, extended, blocks, steps, sems, step_sems
 ):
     leaf_count, count, points, _ = blocks.shape
-    col, row, rows, cols = place[0], place[1], place[2], place[3]
+    col = place[0]
     edge = 2 * REACH
     group = leaf_count // sems.shape[0]
     fetched = [
@@ -181,13 +200,11 @@
     for copy in small + fetched:
         copy.start()
     odd = (col & 1) == 1
-    lowest = (col == 0) & (row == 0)
-    highest = (col == cols - 1) & (row == rows - 1)
     before = jnp.where(odd, second[:edge], first[:edge])
     after = jnp.where(odd, first[:edge], second[:edge])
     extended[edge : edge + 2 * leaf_count] = ordered[...]
-    extended[:edge] = jnp.where(lowest, jnp.zeros_like(before), before)
-    extended[edge + 2 * leaf_count :] = jnp.where(highest, jnp.zeros_like(after), after)
+    extended[:edge] = before * ends[0]
+    extended[edge + 2 * leaf_count :] = after * ends[1]
     for i in range(leaf_count):
         if i % group == 0:
             fetched[i // group].wait()
@@ -213,7 +230,7 @@
     return pl.pallas_call(
         near_kernel,
         out_shape=jax.ShapeDtypeStruct((leaf_count + 1, rhs, points), F32),
-        in_specs=[SMEM, SMEM] + [VMEM] * 3 + [ANY] * 2,
+        in_specs=[SMEM, SMEM] + [VMEM] * 4 + [ANY] * 2,
         out_specs=VMEM,
         scratch_shapes=[
             pltpu.VMEM((2 * leaf_count + 4 * REACH, rhs, LANES), BF),
@@ -225,7 +242,7 @@
         compiler_params=pltpu.CompilerParams(vmem_limit_bytes=24 << 20),
         cost_estimate=pl.CostEstimate(flops=1 << 30, bytes_accessed=1 << 20, transcendentals=0),
         name="near",
-    )(place, offsets, ordered, first, second, in_hbm(near_blocks), in_hbm(up_transfer))
+    )(place, offsets, ends_call(place, rhs), ordered, first, second, in_hbm(near_blocks), in_hbm(up_transfer))
 
 
 def down_kernel(

time: 43.8 us -> 44.4 us (1.014)
  the two profiles are of different devices: /device:TPU:7 before, /device:TPU:16 now
where the time goes in v3:
time: 44.4 us; the launch traced here: 44.1 us
  starting transfers between devices  27.4 us (62%)
  Pallas kernels  14.3 us (32%)
  local copies, waits for them, and re-layouts  2.03 us (5%)
    all_to_all x1, starting transfers between devices, local(): row_poles = lax.all_to_all(row_wire, 'row', 0, 0, tiled=True)  8.58 us
    all_to_all x1, starting transfers between devices, local(): everyone = lax.all_to_all(lifted, 'col', 0, 0, tiled=True)  7.28 us
    ppermute x2, starting transfers between devices, swap(): lax.ppermute(value, ('row', 'col'), pairs + [(b, a) for a, b in pairs])  5.04 us
    pallas_call x1, Pallas kernels, near_call(): pl.pallas_call(near_kernel, out_shape=jax.ShapeDtypeStruct((leaf_count +...  4.65 us
    pallas_call x1, Pallas kernels, up_call(): pl.pallas_call(up_kernel, out_shape=(shape((cols, rhs // 2, LANES), F32),...  4.62 us
    pallas_call x1, Pallas kernels, down_call(): pl.pallas_call(down_kernel, out_shape=jax.ShapeDtypeStruct((rhs, leaf_cou...  3.65 us
    ppermute x2, starting transfers between devices, from_peer(): lax.ppermute(value, 'col', [((c + away) % cols, c) for c in range(cols)])  3.53 us
    ppermute x1, starting transfers between devices, local(): around = lax.ppermute(first[2 * REACH:], ('row', 'col'), turn)  2.97 us
  transfers between devices with their start and end apart: 7, of which 0 were waited for; matrix products, arithmetic and copies ran while one was open for 2% of the time, Pallas kernels for 14%

profile of v3, /device:TPU:16, one launch (start us, length us, event | category | flops | bytes accessed | tf_op | source)
XLA Modules:
  0.0 44.1 jit_solution(4192250152618676935)
XLA Ops:
  0.0 0.1 pad_add_fusion.place
  0.1 4.6 %up.3 = (f32[16,16,128]{2,1,0:T(8,128)}, bf16[16,32,128]{2,1,0:T(8,128)(2,1)S(1)}, bf16[16,32,128]{2,1,0:T(8,128)(2,1)S(1)}, bf16[8,32,128]{2,1,0:T(8,128)(2,1)}, bf16[32,32,128]{2,1,0:T(8,128)(2,1)S(1)}) custom-call(s32[4]{0:T(128)S(1)} %pad_add_fusion.place, bf16[32,4096]{1,0:T(8,128)(2,1)} %x_hbm.1, s32[1,4096]{1,0:T(1,128)} %bitcast.5, ...), custom_call_target="tpu_custom_call" | custom-call | flops 4294967296 | bytes 3145728 | tf_op jit(solution)/shard_map/up/pallas_call | solution.py:141
  4.7 7.3 %all-to-all-start = ((f32[16,16,128]{2,1,0:T(8,128)}), f32[16,16,128]{2,1,0:T(8,128)S(1)}, u32[]{:S(2)}, u32[]{:S(2)}) async-start(f32[16,16,128]{2,1,0:T(8,128)} %get-tuple-element.13), calls=%async_computation | async-start | bytes 262144 | tf_op jit(solution)/shard_map/all_to_all | solution.py:363
  12.0 3.0 %collective-permute-start.3 = (bf16[8,32,128]{2,1,0:T(8,128)(2,1)}, bf16[8,32,128]{2,1,0:T(8,128)(2,1)S(1)}, u32[]{:S(2)}, u32[]{:S(2)}) collective-permute-start(bf16[8,32,128]{2,1,0:T(8,128)(2,1)} %get-tuple-element.12), channel_id=1, source_target_pairs={{8,0},{9,1},{10,2},{11,3},{12,4},{13,5},{14,6},{15,7},{0,8},{1,9},... | collective-permute-start | bytes 196616 | tf_op jit(solution)/shard_map/ppermute | solution.py:370
  15.0 0.6 %collective-permute-start.4 = (bf16[8,32,128]{2,1,0:T(8,128)(2,1)}, bf16[8,32,128]{2,1,0:T(8,128)(2,1)S(1)}, u32[]{:S(2)}, u32[]{:S(2)}) collective-permute-start(bf16[8,32,128]{2,1,0:T(8,128)(2,1)} %get-tuple-element.12), channel_id=1, source_target_pairs={{2,0},{3,1},{4,2},{5,3},{6,4},{7,5},{8,6},{9,7},{10,8},{11,9},{12,... | collective-permute-start | bytes 196616 | tf_op jit(solution)/shard_map/ppermute | solution.py:370
  15.5 2.7 %collective-permute-start = (bf16[16,32,128]{2,1,0:T(8,128)(2,1)S(1)}, bf16[16,32,128]{2,1,0:T(8,128)(2,1)S(1)}, u32[]{:S(2)}, u32[]{:S(2)}) collective-permute-start(bf16[16,32,128]{2,1,0:T(8,128)(2,1)S(1)} %get-tuple-element.10), channel_id=1, source_target_pairs={{1,2},{3,4},{5,6},{7,8},{9,10},{11,12},{13,14},{15,16},{17,18},{19... | collective-permute-start | bytes 393224 | tf_op jit(solution)/shard_map/ppermute | solution.py:367
  18.2 2.4 %collective-permute-start.1 = (bf16[16,32,128]{2,1,0:T(8,128)(2,1)S(1)}, bf16[16,32,128]{2,1,0:T(8,128)(2,1)S(1)}, u32[]{:S(2)}, u32[]{:S(2)}) collective-permute-start(bf16[16,32,128]{2,1,0:T(8,128)(2,1)S(1)} %get-tuple-element.11), channel_id=1, source_target_pairs={{0,1},{2,3},{4,5},{6,7},{8,9},{10,11},{12,13},{14,15},{16,17},{18,... | collective-permute-start | bytes 393224 | tf_op jit(solution)/shard_map/ppermute | solution.py:367
  20.6 0.0 all-to-all-done
  20.6 0.6 %broadcast_in_dim.2 = bf16[16,16,128]{2,1,0:T(8,128)(2,1)} broadcast(bf16[16,128]{1,0:T(8,128)(2,1)S(1)} %reduce_sum.9), dimensions={1,2} | broadcast | bytes 69632 | tf_op jit(solution)/shard_map/broadcast_in_dim | solution.py:374
  21.2 8.6 %all-to-all-start.1 = ((bf16[16,16,128]{2,1,0:T(8,128)(2,1)}), bf16[16,16,128]{2,1,0:T(8,128)(2,1)S(1)}, u32[]{:S(2)}, u32[]{:S(2)}) async-start(bf16[16,16,128]{2,1,0:T(8,128)(2,1)} %broadcast_in_dim.2), calls=%async_computation.1 | async-start | bytes 131072 | tf_op jit(solution)/shard_map/all_to_all | solution.py:375
  29.8 0.0 copy-start
  29.8 0.0 copy-start.1
  29.9 0.0 copy-start.2
  29.9 0.0 copy-start.3
  29.9 0.0 copy-start.4
  29.9 0.0 copy-start.10
  29.9 0.0 copy-start.11
  29.9 1.4 %ends.1 = bf16[2,32,128]{2,1,0:T(8,128)(2,1)} custom-call(s32[4]{0:T(128)} %copy-done.6), custom_call_target="tpu_custom_call" | custom-call | flops 2147483648 | bytes 16384 | tf_op jit(solution)/shard_map/ends/pallas_call | solution.py:176
  31.3 0.0 collective-permute-done.first
  31.3 3.0 %collective-permute-start.2 = (bf16[8,32,128]{2,1,0:T(8,128)(2,1)S(1)}, bf16[8,32,128]{2,1,0:T(8,128)(2,1)S(1)}, u32[]{:S(2)}, u32[]{:S(2)}) collective-permute-start(bf16[8,32,128]{2,1,0:T(8,128)(2,1)S(1)} %slice.4), channel_id=1, source_target_pairs={{16,0},{17,1},{18,2},{19,3},{20,4},{21,5},{22,6},{23,7},{32,16},{3... | collective-permute-start | bytes 196616 | tf_op jit(solution)/shard_map/ppermute | solution.py:382
  34.3 0.7 %copy-done.5 = bf16[2,32,128]{2,1,0:T(8,128)(2,1)S(1)} copy-done((bf16[2,32,128]{2,1,0:T(8,128)(2,1)S(1)}, bf16[2,32,128]{2,1,0:T(8,128)(2,1)}, u32[]{:S(2)}) %copy-start.5) | copy-done | bytes 16408
  35.0 0.6 %copy-done.7 = s32[4]{0:T(128)S(1)} copy-done((s32[4]{0:T(128)S(1)}, s32[4]{0:T(128)}, u32[]{:S(2)}) %copy-start.7) | copy-done | bytes 40
  35.6 4.7 %near.1 = f32[17,32,256]{2,1,0:T(8,128)S(1)} custom-call(s32[4]{0:T(128)S(1)} %copy-done.7, s32[4,16]{1,0:T(4,128)S(1)} %bitcast.7, bf16[2,32,128]{2,1,0:T(8,128)(2,1)S(1)} %copy-done.5, bf16[32,32,128]{2,1,0:T(8,128)(2,1)S(1)} %get-tuple-element.14.ordered, bf16[16,32,128]{2,1,0:T(8,128)(2,1)S(1)} %collective-permute-done.first, ...), custom_call_target="tpu_custom_call" | custom-call | flops 1073741824 | bytes 1048576 | tf_op jit(solution)/shard_map/near/pallas_call | solution.py:230
  40.4 3.6 %down.1 = bf16[32,4096]{1,0:T(8,128)(2,1)} custom-call(s32[4]{0:T(128)S(1)} %copy-done.8, s32[4,16]{1,0:T(4,128)S(1)} %bitcast.8, s32[1,3]{1,0:T(1,128)S(1)} %copy-done.11, bf16[16,32,128]{2,1,0:T(8,128)(2,1)S(1)} %collective-permute-done.first, bf16[16,32,128]{2,1,0:T(8,128)(2,1)S(1)} %collective-permute-done.1.second, ...), custom_call_target="tpu_custom_call" | custom-call | flops 268435456 | bytes 3145728 | tf_op jit(solution)/shard_map/down/pallas_call | solution.py:323
  (23 shorter events, 0.1 us)
Async XLA Ops:
  0.1 29.7 %copy-start.6 = (s32[4]{0:T(128)}, s32[4]{0:T(128)S(1)}, u32[]{:S(2)}) copy-start(s32[4]{0:T(128)S(1)} %pad_add_fusion.place) | copy-start | bytes 52
  0.1 34.2 %copy-start.9 = (s32[16,4]{0,1:T(4,128)S(1)}, s32[16,4]{0,1:T(4,128)}, u32[]{:S(2)}) copy-start(s32[16,4]{0,1:T(4,128)} %param.21) | copy-start | bytes 772
  4.7 15.9 %all-to-all-start = ((f32[16,16,128]{2,1,0:T(8,128)}), f32[16,16,128]{2,1,0:T(8,128)S(1)}, u32[]{:S(2)}, u32[]{:S(2)}) async-start(f32[16,16,128]{2,1,0:T(8,128)} %get-tuple-element.13), calls=%async_computation | async-start | bytes 262144 | tf_op jit(solution)/shard_map/all_to_all | solution.py:363
  12.0 28.3 %collective-permute-start.3 = (bf16[8,32,128]{2,1,0:T(8,128)(2,1)}, bf16[8,32,128]{2,1,0:T(8,128)(2,1)S(1)}, u32[]{:S(2)}, u32[]{:S(2)}) collective-permute-start(bf16[8,32,128]{2,1,0:T(8,128)(2,1)} %get-tuple-element.12), channel_id=1, source_target_pairs={{8,0},{9,1},{10,2},{11,3},{12,4},{13,5},{14,6},{15,7},{0,8},{1,9},... | collective-permute-start | bytes 196616 | tf_op jit(solution)/shard_map/ppermute | solution.py:370
  15.0 25.3 %collective-permute-start.4 = (bf16[8,32,128]{2,1,0:T(8,128)(2,1)}, bf16[8,32,128]{2,1,0:T(8,128)(2,1)S(1)}, u32[]{:S(2)}, u32[]{:S(2)}) collective-permute-start(bf16[8,32,128]{2,1,0:T(8,128)(2,1)} %get-tuple-element.12), channel_id=1, source_target_pairs={{2,0},{3,1},{4,2},{5,3},{6,4},{7,5},{8,6},{9,7},{10,8},{11,9},{12,... | collective-permute-start | bytes 196616 | tf_op jit(solution)/shard_map/ppermute | solution.py:370
  15.5 15.8 %collective-permute-start = (bf16[16,32,128]{2,1,0:T(8,128)(2,1)S(1)}, bf16[16,32,128]{2,1,0:T(8,128)(2,1)S(1)}, u32[]{:S(2)}, u32[]{:S(2)}) collective-permute-start(bf16[16,32,128]{2,1,0:T(8,128)(2,1)S(1)} %get-tuple-element.10), channel_id=1, source_target_pairs={{1,2},{3,4},{5,6},{7,8},{9,10},{11,12},{13,14},{15,16},{17,18},{19... | collective-permute-start | bytes 393224 | tf_op jit(solution)/shard_map/ppermute | solution.py:367
  18.2 16.1 %collective-permute-start.1 = (bf16[16,32,128]{2,1,0:T(8,128)(2,1)S(1)}, bf16[16,32,128]{2,1,0:T(8,128)(2,1)S(1)}, u32[]{:S(2)}, u32[]{:S(2)}) collective-permute-start(bf16[16,32,128]{2,1,0:T(8,128)(2,1)S(1)} %get-tuple-element.11), channel_id=1, source_target_pairs={{0,1},{2,3},{4,5},{6,7},{8,9},{10,11},{12,13},{14,15},{16,17},{18,... | collective-permute-start | bytes 393224 | tf_op jit(solution)/shard_map/ppermute | solution.py:367
  21.2 19.1 %all-to-all-start.1 = ((bf16[16,16,128]{2,1,0:T(8,128)(2,1)}), bf16[16,16,128]{2,1,0:T(8,128)(2,1)S(1)}, u32[]{:S(2)}, u32[]{:S(2)}) async-start(bf16[16,16,128]{2,1,0:T(8,128)(2,1)} %broadcast_in_dim.2), calls=%async_computation.1 | async-start | bytes 131072 | tf_op jit(solution)/shard_map/all_to_all | solution.py:375
  29.8 10.5 %copy-start = (bf16[16,4,64,64]{3,2,1,0:T(8,128)(2,1)S(1)}, bf16[16,4,64,64]{3,2,1,0:T(8,128)(2,1)}, u32[]{:S(2)}) copy-start(bf16[16,4,64,64]{3,2,1,0:T(8,128)(2,1)} %couple.1) | copy-start | bytes 1572868
  29.8 10.5 %copy-start.1 = (bf16[16,64,256]{2,1,0:T(8,128)(2,1)S(1)}, bf16[16,64,256]{2,1,0:T(8,128)(2,1)}, u32[]{:S(2)}) copy-start(bf16[16,64,256]{2,1,0:T(8,128)(2,1)} %basis.1) | copy-start | bytes 1572868
  29.9 10.5 %copy-start.2 = (f32[16,64,64]{2,1,0:T(8,128)S(1)}, f32[16,64,64]{2,1,0:T(8,128)}, u32[]{:S(2)}) copy-start(f32[16,64,64]{2,1,0:T(8,128)} %leaf_up.1) | copy-start | bytes 786436
  29.9 10.5 %copy-start.3 = (bf16[1,3,64,64]{3,2,1,0:T(8,128)(2,1)S(1)}, bf16[1,3,64,64]{3,2,1,0:T(8,128)(2,1)}, u32[]{:S(2)}) copy-start(bf16[1,3,64,64]{3,2,1,0:T(8,128)(2,1)} %couple_row.1) | copy-start | bytes 73732
  29.9 10.5 %copy-start.4 = (s32[4096]{0:T(1024)S(1)}, s32[4096]{0:T(1024)}, u32[]{:S(2)}) copy-start(s32[4096]{0:T(1024)} %param.12) | copy-start | bytes 49156
  29.9 10.5 %copy-start.10 = (s32[16,4]{0,1:T(4,128)S(1)}, s32[16,4]{0,1:T(4,128)}, u32[]{:S(2)}) copy-start(s32[16,4]{0,1:T(4,128)} %param.17) | copy-start | bytes 772
  29.9 10.5 %copy-start.11 = (s32[1,3]{1,0:T(1,128)S(1)}, s32[1,3]{1,0:T(1,128)}, u32[]{:S(2)}) copy-start(s32[1,3]{1,0:T(1,128)} %row_lists.1) | copy-start | bytes 40
  31.3 9.1 %copy-start.8 = (s32[4]{0:T(128)S(1)}, s32[4]{0:T(128)}, u32[]{:S(2)}) copy-start(s32[4]{0:T(128)} %copy-done.6) | copy-start | bytes 52
  31.3 9.0 %collective-permute-start.2 = (bf16[8,32,128]{2,1,0:T(8,128)(2,1)S(1)}, bf16[8,32,128]{2,1,0:T(8,128)(2,1)S(1)}, u32[]{:S(2)}, u32[]{:S(2)}) collective-permute-start(bf16[8,32,128]{2,1,0:T(8,128)(2,1)S(1)} %slice.4), channel_id=1, source_target_pairs={{16,0},{17,1},{18,2},{19,3},{20,4},{21,5},{22,6},{23,7},{32,16},{3... | collective-permute-start | bytes 196616 | tf_op jit(solution)/shard_map/ppermute | solution.py:382
  34.3 0.7 %copy-start.5 = (bf16[2,32,128]{2,1,0:T(8,128)(2,1)S(1)}, bf16[2,32,128]{2,1,0:T(8,128)(2,1)}, u32[]{:S(2)}) copy-start(bf16[2,32,128]{2,1,0:T(8,128)(2,1)} %ends.1) | copy-start | bytes 49156
  35.0 0.6 %copy-start.7 = (s32[4]{0:T(128)S(1)}, s32[4]{0:T(128)}, u32[]{:S(2)}) copy-start(s32[4]{0:T(128)} %copy-done.6) | copy-start | bytes 52
